TPU v7x, 32 devices: a whole 2x2x4 slice. The times are simulated.
32 devices in a mesh: dp: 4 (over z), expert: 2 (over x), tensor: 4 (over y, core).
Axes of the slice: x: 2, y: 2, z: 4, core: 2. Of those that a mesh axis runs over, the one named last changes fastest.
Arguments:
- hidden_in: bfloat16 [16384, 768], P(('dp', 'expert')), may hold values from -6 to 6
- prev_logits: bfloat16 [16384, 6], P(('dp', 'expert')), may hold values from -4 to 4
- routes: int32 [16384, 2], P(('dp', 'expert')), may hold values from 0 to 5, all different within a row; in each aligned block of 2048 rows (0 to 2047, 2048 to 4095, ...) at most 1024 rows name the same one
- block_ids: int32 [8, 2048], P(('dp', 'expert')), may hold values from 0 to 11, never falling along the last dimension, each value on 1 to 256 neighbouring positions
- cotangent: bfloat16 [16384, 768], P(('dp', 'expert')), may hold values from -6 to 6
- gain_attn: bfloat16 [768], replicated, may hold values from 0.5 to 1.5
- w_qkv: bfloat16 [768, 2304], P(None, 'tensor'), may hold values from -0.21875 to 0.21875
- w_out: bfloat16 [768, 768], P('tensor'), may hold values from -3 to 3
- gain_moe: bfloat16 [768], replicated, may hold values from 0.5 to 1.5
- w_router: bfloat16 [768, 6], replicated, may hold values from -0.15625 to 0.15625
- w_prev: bfloat16 [6, 6], replicated, may hold values from -2.5 to 2.5
- w_const: bfloat16 [2, 768, 2], replicated, may hold values from -0.21875 to 0.21875
- v_const: bfloat16 [2, 768], replicated, may hold values from -16 to 16
- w_gate_up: bfloat16 [2, 768, 2, 2048], P('expert', None, None, 'tensor'), may hold values from -0.21875 to 0.21875
- w_down: bfloat16 [2, 2048, 768], P('expert', 'tensor'), may hold values from -1.25 to 1.25
Outputs:
- output: float32 [16384, 768], P(('dp', 'expert'))
- grad_input: float32 [16384, 768], P(('dp', 'expert'))
- grad_prev: float32 [16384, 6], P(('dp', 'expert'))
- grad_gain_attn: float32 [768], replicated
- grad_qkv: float32 [768, 2304], P(('dp', 'expert'), 'tensor')
- grad_out: float32 [768, 768], P('tensor', ('dp', 'expert'))
- grad_gain_moe: float32 [768], replicated
- grad_router: float32 [768, 6], replicated
- grad_prev_weight: float32 [6, 6], replicated
- grad_const_weight: float32 [2, 768, 2], replicated
- grad_const_vector: float32 [2, 768], replicated
- grad_gate_up: float32 [2, 768, 2, 2048], P('expert', 'dp', None, 'tensor')
- grad_down: float32 [2, 2048, 768], P('expert', 'tensor', 'dp')
- loss: float32 [], replicated
- expert_load: float32 [2, 6], replicated
Inputs may be any that keep to these rules, and one draw needn't show every extreme that they name: Within the 2048 rows of one device no expert is named by more than 1024 routes, a bound that some block reaches; the two experts of a token differ. `block_ids`: within a sequence block ids never fall, each block has 1 to 256 positions, and one has exactly 256.
All inputs are finite; a program needn't handle non-finite values.
Results may differ from a plain program's by a relative error of at most 0.023.
Values may be sent and summed in bfloat16 or wider, within the bound.
A program may use at most 320 MiB of HBM per device.

v0:
```python
import jax
import jax.numpy as jnp
from jax import lax
from jax.sharding import PartitionSpec as P

HEAD_DIM = 64


EPSILON = 1e-06
AUX_WEIGHT = 0.01
QUERY_BLOCK = 512
SCORE_SCALE = 0.125


def rms_factor(values):
    return lax.rsqrt(jnp.mean(values * values, axis=-1, keepdims=True) + EPSILON)


def plain_dot(left_side, right_side):
    return jnp.dot(left_side, right_side, preferred_element_type=jnp.float32)


def inner_rows(left_side, right_side):
    return lax.dot_general(
        left_side, right_side, (((0,), (0,)), ((), ())), preferred_element_type=jnp.float32
    )


def exact_inner_rows(left_side, right_side):
    return lax.dot_general(
        left_side,
        right_side,
        (((0,), (0,)), ((), ())),
        precision=lax.Precision.HIGHEST,
        preferred_element_type=jnp.float32,
    )


def outer_cols(left_side, right_side):
    return lax.dot_general(
        left_side, right_side, (((1,), (1,)), ((), ())), preferred_element_type=jnp.float32
    )


def exact_outer_cols(left_side, right_side):
    return lax.dot_general(
        left_side,
        right_side,
        (((1,), (1,)), ((), ())),
        precision=lax.Precision.HIGHEST,
        preferred_element_type=jnp.float32,
    )


def masked_scores(query_part, key_rows, query_blocks, key_blocks):
    scores = (
        jnp.einsum("qhd,khd->hqk", query_part, key_rows, preferred_element_type=jnp.float32)
        * SCORE_SCALE
    )
    allowed = key_blocks[None, None, :] <= query_blocks[None, :, None]
    return jnp.where(allowed, scores, -1e30)


def attend_forward(queries, key_rows, value_rows, block_row, block_rows):
    block_count = queries.shape[0] // block_rows

    def one_block(block_index):
        block_start = block_index * block_rows
        query_part = lax.dynamic_slice_in_dim(queries, block_start, block_rows, 0)
        query_blocks = lax.dynamic_slice_in_dim(block_row, block_start, block_rows, 0)
        scores = masked_scores(query_part, key_rows, query_blocks, block_row)
        top_score = jnp.max(scores, axis=-1, keepdims=True)
        expanded = jnp.exp(scores - top_score)
        total_mass = jnp.sum(expanded, axis=-1, keepdims=True)
        weights = (expanded / total_mass).astype(jnp.bfloat16)
        mixed_part = jnp.einsum(
            "hqk,khd->qhd", weights, value_rows, preferred_element_type=jnp.float32
        )
        return (mixed_part.astype(jnp.bfloat16), (top_score + jnp.log(total_mass))[..., 0])

    mixed_parts, log_mass = lax.map(one_block, jnp.arange(block_count, dtype=jnp.int32))
    return (mixed_parts.reshape(queries.shape), log_mass)


def attend_backward(queries, key_rows, value_rows, block_row, log_mass, grad_mixed, block_rows):
    block_count = queries.shape[0] // block_rows
    zero_grads = jnp.zeros(key_rows.shape, jnp.float32)

    def one_block(grad_carry, inputs_now):
        block_index, mass_part = inputs_now
        grad_keys, grad_values = grad_carry
        block_start = block_index * block_rows
        query_part = lax.dynamic_slice_in_dim(queries, block_start, block_rows, 0)
        query_blocks = lax.dynamic_slice_in_dim(block_row, block_start, block_rows, 0)
        grad_part = lax.dynamic_slice_in_dim(grad_mixed, block_start, block_rows, 0)
        scores = masked_scores(query_part, key_rows, query_blocks, block_row)
        weights = jnp.exp(scores - mass_part[:, :, None])
        grad_values = grad_values + jnp.einsum(
            "hqk,qhd->khd",
            weights.astype(jnp.bfloat16),
            grad_part,
            preferred_element_type=jnp.float32,
        )
        grad_weights = jnp.einsum(
            "qhd,khd->hqk", grad_part, value_rows, preferred_element_type=jnp.float32
        )
        inner_total = jnp.sum(weights * grad_weights, axis=-1, keepdims=True)
        grad_scores = (weights * (grad_weights - inner_total)).astype(jnp.bfloat16)
        grad_queries = (
            jnp.einsum("hqk,khd->qhd", grad_scores, key_rows, preferred_element_type=jnp.float32)
            * SCORE_SCALE
        )
        grad_keys = (
            grad_keys
            + jnp.einsum(
                "hqk,qhd->khd", grad_scores, query_part, preferred_element_type=jnp.float32
            )
            * SCORE_SCALE
        )
        return ((grad_keys, grad_values), grad_queries)

    (grad_keys, grad_values), grad_queries = lax.scan(
        one_block, (zero_grads, zero_grads), (jnp.arange(block_count, dtype=jnp.int32), log_mass)
    )
    grad_queries = grad_queries.reshape(key_rows.shape)
    return jnp.stack([grad_queries, grad_keys, grad_values], axis=2)


def route_slots(group_routes, expert_count, capacity, type_count):
    flat_routes = group_routes.reshape(-1)
    one_hot = (flat_routes[:, None] == jnp.arange(type_count, dtype=jnp.int32)[None, :]).astype(
        jnp.int32
    )
    ranks = jnp.cumsum(one_hot, axis=0) - 1
    slots = jnp.sum(ranks * one_hot, axis=1)
    return jnp.where(
        flat_routes < expert_count, flat_routes * capacity + slots, expert_count * capacity
    )


def expert_inner(expert_rows, weights_gate_up):
    gate_up = jnp.einsum(
        "rd,dgf->rgf", expert_rows, weights_gate_up, preferred_element_type=jnp.float32
    )
    hidden = (jax.nn.silu(gate_up[:, 0]) * gate_up[:, 1]).astype(jnp.bfloat16)
    return (gate_up, hidden)


def expert_backward(expert_rows, weights_gate_up, weights_down, gate_up, hidden, grad_result):
    grad_hidden = outer_cols(grad_result, weights_down)
    grad_weights_down = inner_rows(hidden, grad_result)
    gate_part = gate_up[:, 0]
    up_part = gate_up[:, 1]
    sigmoid = jax.nn.sigmoid(gate_part)
    grad_gate = grad_hidden * up_part * sigmoid * (1.0 + gate_part * (1.0 - sigmoid))
    grad_up = grad_hidden * gate_part * sigmoid
    grad_gate_up = jnp.stack([grad_gate, grad_up], axis=1).astype(jnp.bfloat16)
    grad_rows = jnp.einsum(
        "rgf,dgf->rd", grad_gate_up, weights_gate_up, preferred_element_type=jnp.float32
    )
    grad_weights_gate_up = jnp.einsum(
        "rd,rgf->dgf", expert_rows, grad_gate_up, preferred_element_type=jnp.float32
    )
    return (grad_rows, grad_weights_gate_up, grad_weights_down)


def per_device(
    hidden_in,
    prev_logits,
    routes,
    block_ids,
    cotangent,
    gain_attn,
    w_qkv,
    w_out,
    gain_moe,
    w_router,
    w_prev,
    w_const,
    v_const,
    w_gate_up,
    w_down,
):
    inputs = hidden_in.astype(jnp.float32)
    tok_rows, model_width = inputs.shape
    seq_count, length = block_ids.shape
    type_count = w_router.shape[1]
    expert_count = lax.axis_size("expert")
    capacity = 3 * tok_rows // type_count // 8 * 8
    local_heads = w_out.shape[0] // HEAD_DIM
    block_rows = min(QUERY_BLOCK, length)
    gain_first = gain_attn.astype(jnp.float32)
    scale_first = rms_factor(inputs)
    normed_first = inputs * scale_first
    normed_in = (normed_first * gain_first).astype(jnp.bfloat16)
    qkv_rows = plain_dot(normed_in, w_qkv).astype(jnp.bfloat16)
    qkv_split = qkv_rows.reshape(seq_count, length, local_heads, 3, HEAD_DIM)
    sequence = 0
    mixed_one, mass_one = attend_forward(
        qkv_split[sequence, :, :, 0],
        qkv_split[sequence, :, :, 1],
        qkv_split[sequence, :, :, 2],
        block_ids[sequence],
        block_rows,
    )
    mixed_list = [mixed_one]
    mass_list = [mass_one]
    mixed_heads = jnp.stack(mixed_list).reshape(tok_rows, local_heads * HEAD_DIM)
    attention_out = lax.psum(plain_dot(mixed_heads, w_out).astype(jnp.bfloat16), "tensor").astype(
        jnp.float32
    )
    residual = inputs + attention_out
    gain_second = gain_moe.astype(jnp.float32)
    scale_second = rms_factor(residual)
    normed_second = residual * scale_second
    moe_in = (normed_second * gain_second).astype(jnp.bfloat16)
    moe_values = moe_in.astype(jnp.float32)
    logits = plain_dot(moe_in, w_router) + plain_dot(prev_logits, w_prev)
    route_probs = jax.nn.softmax(logits, axis=-1)
    type_ids = jnp.arange(type_count, dtype=jnp.int32)
    choose = (routes[:, :, None] == type_ids[None, None, :]).astype(jnp.float32)
    gate_values = jnp.sum(choose * route_probs[:, None, :], axis=-1)
    count_all, prob_all = lax.psum(
        (jnp.sum(choose, axis=(0, 1)), jnp.sum(route_probs, axis=0)), ("dp", "expert")
    )
    token_total = tok_rows * lax.axis_size(("dp", "expert"))
    load_share = count_all / (2.0 * token_total)
    balance_loss = type_count * jnp.sum(load_share * prob_all / token_total)
    load_stats = jnp.stack([count_all / (2.0 * tok_rows), prob_all / tok_rows])
    destination = route_slots(routes, expert_count, capacity, type_count)
    buffer_in = (
        jnp.zeros((expert_count * capacity + 1, model_width), jnp.bfloat16)
        .at[destination]
        .set(jnp.repeat(moe_in, 2, axis=0))
    )
    buffer_in = buffer_in[:-1].reshape(expert_count, capacity, model_width)
    weights_gate_up = w_gate_up[0]
    weights_down = w_down[0]

    def send_out(buffer):
        received = lax.all_to_all(buffer, "expert", split_axis=0, concat_axis=0, tiled=True)
        return received.reshape(-1, model_width)

    def send_back(expert_result):
        shaped = expert_result.reshape(expert_count, -1, model_width)
        sent_part = lax.psum_scatter(
            shaped.astype(jnp.bfloat16), "tensor", scatter_dimension=2, tiled=True
        )
        returned = lax.all_to_all(sent_part, "expert", split_axis=0, concat_axis=0, tiled=True)
        return lax.all_gather(returned, "tensor", axis=2, tiled=True)

    expert_rows = send_out(buffer_in)
    gate_up, hidden = expert_inner(expert_rows, weights_gate_up)
    expert_out = send_back(plain_dot(hidden, weights_down))
    zero_row = jnp.zeros((1, model_width), jnp.bfloat16)
    out_table = jnp.concatenate([expert_out.reshape(-1, model_width), zero_row], axis=0)
    ffn_values = (
        jnp.take(out_table, destination, axis=0)
        .astype(jnp.float32)
        .reshape(tok_rows, 2, model_width)
    )
    const_logits = jnp.einsum("td,cdk->tck", moe_in, w_const, preferred_element_type=jnp.float32)
    const_mix = jax.nn.softmax(const_logits, axis=-1)
    const_vectors = v_const.astype(jnp.float32)
    const_values = (
        const_mix[:, :, 0:1] * moe_values[:, None, :] + const_mix[:, :, 1:2] * const_vectors[None]
    )
    copy_mask = choose[:, :, expert_count + 1]
    first_const = choose[:, :, expert_count + 2]
    second_const = choose[:, :, expert_count + 3]
    route_values = ffn_values + copy_mask[..., None] * moe_values[:, None, :]
    route_values = (
        route_values
        + first_const[..., None] * const_values[:, None, 0]
        + second_const[..., None] * const_values[:, None, 1]
    )
    output = residual + jnp.sum(gate_values[..., None] * route_values, axis=1)
    grad_result = cotangent.astype(jnp.float32)
    grad_gates = jnp.sum(grad_result[:, None, :] * route_values, axis=-1)
    grad_routes = (
        (gate_values[..., None] * grad_result[:, None, :])
        .astype(jnp.bfloat16)
        .reshape(-1, model_width)
    )
    grad_buffer = (
        jnp.zeros((expert_count * capacity + 1, model_width), jnp.bfloat16)
        .at[destination]
        .set(grad_routes)
    )
    grad_buffer = grad_buffer[:-1].reshape(expert_count, capacity, model_width)
    grad_expert_in = send_out(grad_buffer)
    gate_up_back, hidden_back = (gate_up, hidden)
    grad_rows, grad_weights_gate_up, grad_weights_down = expert_backward(
        expert_rows, weights_gate_up, weights_down, gate_up_back, hidden_back, grad_expert_in
    )
    grad_returned = send_back(grad_rows)
    grad_table = jnp.concatenate([grad_returned.reshape(-1, model_width), zero_row], axis=0)
    grad_moe = jnp.sum(
        jnp.take(grad_table, destination, axis=0)
        .astype(jnp.float32)
        .reshape(tok_rows, 2, model_width),
        axis=1,
    )
    copy_gate = jnp.sum(gate_values * copy_mask, axis=1)
    grad_moe = grad_moe + copy_gate[:, None] * grad_result
    const_gate = jnp.stack(
        [jnp.sum(gate_values * first_const, axis=1), jnp.sum(gate_values * second_const, axis=1)],
        axis=1,
    )
    grad_const_out = const_gate[:, :, None] * grad_result[:, None, :]
    grad_mix = jnp.stack(
        [
            jnp.sum(grad_const_out * moe_values[:, None, :], axis=-1),
            jnp.sum(grad_const_out * const_vectors[None], axis=-1),
        ],
        axis=-1,
    )
    grad_const_logits = const_mix * (
        grad_mix - jnp.sum(const_mix * grad_mix, axis=-1, keepdims=True)
    )
    grad_moe = grad_moe + jnp.sum(const_mix[:, :, 0:1] * grad_const_out, axis=1)
    grad_moe = grad_moe + jnp.einsum(
        "tck,cdk->td",
        grad_const_logits,
        w_const.astype(jnp.float32),
        precision=lax.Precision.HIGHEST,
        preferred_element_type=jnp.float32,
    )
    grad_w_const = jnp.einsum(
        "td,tck->cdk",
        moe_values,
        grad_const_logits,
        precision=lax.Precision.HIGHEST,
        preferred_element_type=jnp.float32,
    )
    grad_v_const = jnp.sum(const_mix[:, :, 1:2] * grad_const_out, axis=0)
    grad_probs = (
        jnp.sum(choose * grad_gates[..., None], axis=1)
        + AUX_WEIGHT * type_count * load_share[None, :] / token_total
    )
    grad_logits = route_probs * (
        grad_probs - jnp.sum(route_probs * grad_probs, axis=-1, keepdims=True)
    )
    grad_router = exact_inner_rows(moe_values, grad_logits)
    prev_values = prev_logits.astype(jnp.float32)
    grad_prev_weight = exact_inner_rows(prev_values, grad_logits)
    grad_prev = exact_outer_cols(grad_logits, w_prev.astype(jnp.float32))
    grad_moe = grad_moe + exact_outer_cols(grad_logits, w_router.astype(jnp.float32))
    grad_gain_moe = jnp.sum(grad_moe * normed_second, axis=0)
    grad_normed_second = grad_moe * gain_second
    grad_residual = grad_result + scale_second * (
        grad_normed_second
        - normed_second * jnp.mean(grad_normed_second * normed_second, axis=-1, keepdims=True)
    )
    grad_attention = grad_residual.astype(jnp.bfloat16)
    grad_w_out = inner_rows(mixed_heads, grad_attention)
    grad_mixed = (
        outer_cols(grad_attention, w_out)
        .astype(jnp.bfloat16)
        .reshape(seq_count, length, local_heads, HEAD_DIM)
    )
    sequence = 0
    grad_list = [
        attend_backward(
            qkv_split[sequence, :, :, 0],
            qkv_split[sequence, :, :, 1],
            qkv_split[sequence, :, :, 2],
            block_ids[sequence],
            mass_list[sequence],
            grad_mixed[sequence],
            block_rows,
        )
    ]
    grad_qkv_rows = jnp.stack(grad_list).reshape(tok_rows, -1).astype(jnp.bfloat16)
    grad_w_qkv = inner_rows(normed_in, grad_qkv_rows)
    grad_first = lax.psum(outer_cols(grad_qkv_rows, w_qkv).astype(jnp.bfloat16), "tensor").astype(
        jnp.float32
    )
    grad_gain_attn = jnp.sum(grad_first * normed_first, axis=0)
    grad_normed_first = grad_first * gain_first
    grad_input = grad_residual + scale_first * (
        grad_normed_first
        - normed_first * jnp.mean(grad_normed_first * normed_first, axis=-1, keepdims=True)
    )
    grad_qkv_sum, grad_out_sum = (
        lax.psum_scatter(grad_w_qkv, ("dp", "expert"), scatter_dimension=0, tiled=True),
        lax.psum_scatter(grad_w_out, ("dp", "expert"), scatter_dimension=1, tiled=True),
    )
    small_sums = lax.psum(
        (grad_gain_attn, grad_gain_moe, grad_router, grad_prev_weight, grad_w_const, grad_v_const),
        ("dp", "expert"),
    )
    grad_gate_up_all = grad_weights_gate_up[None]
    grad_down_all = grad_weights_down[None]
    grad_gate_up_sum, grad_down_sum = (
        lax.psum_scatter(
            grad_gate_up_all.astype(jnp.bfloat16), "dp", scatter_dimension=1, tiled=True
        ).astype(jnp.float32),
        lax.psum_scatter(
            grad_down_all.astype(jnp.bfloat16), "dp", scatter_dimension=2, tiled=True
        ).astype(jnp.float32),
    )
    return (
        output,
        grad_input,
        grad_prev,
        small_sums[0],
        grad_qkv_sum,
        grad_out_sum,
        small_sums[1],
        small_sums[2],
        small_sums[3],
        small_sums[4],
        small_sums[5],
        grad_gate_up_sum,
        grad_down_sum,
        balance_loss,
        load_stats,
    )


def solution(mesh):
    return jax.shard_map(
        per_device,
        mesh=mesh,
        in_specs=(
            P(("dp", "expert"), None),
            P(("dp", "expert"), None),
            P(("dp", "expert"), None),
            P(("dp", "expert"), None),
            P(("dp", "expert"), None),
            P(),
            P(None, "tensor"),
            P("tensor", None),
            P(),
            P(),
            P(),
            P(),
            P(),
            P("expert", None, None, "tensor"),
            P("expert", "tensor", None),
        ),
        out_specs=(
            P(("dp", "expert"), None),
            P(("dp", "expert"), None),
            P(("dp", "expert"), None),
            P(),
            P(("dp", "expert"), "tensor"),
            P("tensor", ("dp", "expert")),
            P(),
            P(),
            P(),
            P(),
            P(),
            P("expert", "dp", None, "tensor"),
            P("expert", "tensor", "dp"),
            P(),
            P(),
        ),
        check_vma=False,
    )
```

profile of v0, /device:TPU:0, one launch (start us, length us, event | category | flops | bytes accessed | tf_op | source)
XLA Modules:
  0.0 1294.1 jit_solution(6989684725480602346)
XLA Ops:
  16.0 93.9 %while.27 = (s32[]{:T(128)}, bf16[4,512,3,64]{1,3,2,0:T(8,128)(2,1)}, f32[4,3,512]{2,1,0:T(4,128)}, s32[1,2048]{1,0:T(1,128)S(1)}, s32[4]{0:T(128)S(1)}, /*index...) while((s32[]{:T(128)}, ...), condition=%wide.region_4.5_spmd, body=%wide.region_1.4_spmd.sunk | while | flops 844200448 | bytes 43974860 | solution.py:81
  124.5 62.9 %all-reduce.6.cloned.1.call-done = bf16[2048,768]{1,0:T(8,128)(2,1)} async-done(((bf16[2048,768]{1,0:T(8,128)(2,1)}), bf16[2048,768]{1,0:T(8,128)(2,1)}) %all-reduce.6.cloned.1.call-update) | async-done | bytes 3145744 | tf_op jit(solution)/shard_map/psum | solution.py:209
  215.7 21.1 %scatter_custom_fusion = bf16[2049,768]{1,0:T(8,128)(2,1)} fusion(s32[4096]{0:T(1024)S(1)} %bitcast.312, bf16[4096,768]{1,0:T(8,128)(2,1)} %reshape.336, bf16[]{:T(256)} %constant.65.clone.1), kind=kCustom, calls=%fused_computation.131 | custom fusion | bytes 3147776 | tf_op jit(solution)/shard_map/scatter | solution.py:234
  238.6 39.1 %all_to_all.20 = bf16[2,1024,768]{2,1,0:T(8,128)(2,1)S(1)} all-to-all(bf16[2,1024,768]{2,1,0:T(8,128)(2,1)S(1)} %bitcast.278), channel_id=1, replica_groups=mesh['dp'=4,'expert'=2,'tensor'=4] {'expert'}, dimensions={0} | all-to-all | bytes 6291456 | tf_op jit(solution)/shard_map/all_to_all | solution.py:241
  303.8 16.0 %mul.450 = f32[4096,768]{1,0:T(8,128)} reshape(f32[2048,2,768]{2,1,0:T(2,128)} %mul.449) | data formatting | bytes 25165824 | tf_op jit(solution)/shard_map/mul | solution.py:281
  389.8 15.8 %mul.480 = f32[4096,768]{1,0:T(8,128)} reshape(f32[2048,2,768]{2,1,0:T(2,128)} %mul.444) | data formatting | bytes 25165824 | tf_op jit(solution)/shard_map/mul | solution.py:275
  414.7 15.8 %mul.476 = f32[4096,768]{1,0:T(8,128)} reshape(f32[2048,2,768]{2,1,0:T(2,128)} %mul.439) | data formatting | bytes 25165824 | tf_op jit(solution)/shard_map/mul | solution.py:274
  441.3 15.8 %mul.472 = f32[4096,768]{1,0:T(8,128)} reshape(f32[2048,2,768]{2,1,0:T(2,128)} %mul.427) | data formatting | bytes 25165824 | tf_op jit(solution)/shard_map/mul | solution.py:271
  468.6 21.4 %gather_fusion = bf16[4096,768]{1,0:T(8,128)(2,1)} fusion(bf16[2049,768]{1,0:T(8,128)(2,1)} %concatenate.6, s32[4096]{0:T(1024)S(1)} %broadcast_clamp_fusion), kind=kCustom, calls=%fused_computation.clone | custom fusion | bytes 12599296 | tf_op jit(solution)/shard_map/jit(_take)/gather | solution.py:258
  490.0 18.9 %multiply_reduce_fusion.1 = f32[4096]{0:T(1024)S(1)} fusion(f32[4096,768]{1,0:T(8,128)} %mul.450, f32[4096,768]{1,0:T(8,128)} %mul.480, f32[4096,768]{1,0:T(8,128)} %mul.476, f32[4096,768]{1,0:T(8,128)} %mul.472, f32[4096]{0:T(1024)S(1)} %mul.478, f32[4096]{0:T(1024)S(1)} %mul.474, f32[4096]{0:T(1024)S(1)} %mul.470, bf16[4096,768]{1,0:T(8,128)(2,1)} %gather_fusion, ...), kind=kLoop, calls=%fused_computation.57 | loop fusion | flops 31453184 | bytes 56692736 | tf_op jit(solution)/shard_map/reduce_sum | solution.py:279
  518.4 22.7 %scatter_custom_fusion.1 = bf16[2049,768]{1,0:T(8,128)(2,1)} fusion(s32[4096]{0:T(1024)} %bitcast.313, f32[4096,768]{1,0:T(8,128)} %mul.450, f32[4096]{0:T(1024)S(1)} %mul.447, bf16[]{:T(256)} %constant.65.clone.1), kind=kCustom, calls=%fused_computation.76 | custom fusion | flops 6291456 | bytes 15747072 | tf_op jit(solution)/shard_map/scatter | solution.py:288
  542.9 36.8 %all_to_all.21 = bf16[2,1024,768]{2,1,0:T(8,128)(2,1)S(1)} all-to-all(bf16[2,1024,768]{2,1,0:T(8,128)(2,1)S(1)} %bitcast.279), channel_id=1, replica_groups=mesh['dp'=4,'expert'=2,'tensor'=4] {'expert'}, dimensions={0} | all-to-all | bytes 6291456 | tf_op jit(solution)/shard_map/all_to_all | solution.py:241
  593.0 38.6 %reduce-scatter.13.cloned.1.call-done = bf16[2,1024,192]{1,2,0:T(8,128)(2,1)} async-done(((bf16[2,1024,768]{1,2,0:T(8,128)(2,1)}), bf16[2,1024,192]{1,2,0:T(8,128)(2,1)}) %reduce-scatter.13.cloned.1.call-update) | async-done | bytes 786448 | tf_op jit(solution)/shard_map/reduce_scatter | solution.py:246
  631.6 15.5 %all_to_all.22 = bf16[2,1024,192]{1,2,0:T(8,128)(2,1)} all-to-all(bf16[2,1024,192]{1,2,0:T(8,128)(2,1)} %reduce-scatter.13.cloned.1.call-done), channel_id=1, replica_groups=mesh['dp'=4,'expert'=2,'tensor'=4] {'expert'}, dimensions={0} | all-to-all | bytes 1572864 | tf_op jit(solution)/shard_map/all_to_all | solution.py:249
  652.2 20.2 %psum.71 = f32[6]{0:T(128)S(1)} all-reduce(f32[6]{0:T(128)S(1)} %get-tuple-element.229), channel_id=1, replica_groups=mesh['dp'=4,'expert'=2,'tensor'=4] {'dp','expert'}, use_global_device_ids=true, to_apply=%region_31.33 | all-reduce | flops 6 | bytes 48 | tf_op jit(solution)/shard_map/psum | solution.py:223
  706.6 21.4 %gather_fusion.1 = bf16[4096,768]{1,0:T(8,128)(2,1)} fusion(bf16[2049,768]{1,0:T(8,128)(2,1)} %concatenate.7, s32[4096]{0:T(1024)S(1)} %broadcast_clamp_fusion), kind=kCustom, calls=%fused_computation.1.clone | custom fusion | bytes 12599296 | tf_op jit(solution)/shard_map/jit(_take)/gather | solution.py:299
  740.8 15.3 %reshape.308 = f32[2048,2,768]{2,1,0:T(2,128)} reshape(f32[4096,768]{1,0:T(8,128)} %get-tuple-element.307) | data formatting | bytes 25165824 | tf_op jit(solution)/shard_map/reshape | solution.py:260
  756.1 81.5 %fusion.41 = (f32[2,768]{1,0:T(2,128)}, f32[2048,2]{1,0:T(8,128)}, f32[2048,2]{1,0:T(8,128)}, f32[2048,768]{1,0:T(8,128)}, f32[2048,768]{1,0:T(8,128)}) fusion(f32[2048,2]{1,0:T(8,128)} %copy.84, f32[2048,768]{1,0:T(8,128)} %convert_element_type.135, f32[2048,2]{1,0:T(8,128)S(1)} %bitcast.285, f32[2,768]{1,0:T(2,128)S(1)} %copy-done.62, ...), kind=kLoop, calls=%fused_computation.56 | loop fusion | flops 50321920 | bytes 50491392 | tf_op jit(solution)/shard_map/reduce_sum | solution.py:336
  856.1 36.9 %reduce_sum.262 = f32[2048,768]{1,0:T(8,128)} reduce(f32[2048,2,768]{2,1,0:T(2,128)} %reshape.315, f32[]{:T(128)} %constant.66.clone.1), dimensions={1}, to_apply=%region_20.22 | reduce | flops 1572864 | bytes 18874372 | tf_op jit(solution)/shard_map/reduce_sum | solution.py:298
  920.3 155.9 %while.28 = (s32[]{:T(128)}, f32[2048,3,64]{0,2,1:T(8,128)}, f32[2048,3,64]{0,2,1:T(8,128)}, bf16[4,512,3,64]{1,3,2,0:T(8,128)(2,1)}, s32[4]{0:T(128)S(1)}, /*in...) while((s32[]{:T(128)}, f32[2048,3,64]{0,2,1:T(8,128)}, ...), condition=%wide.region_36.38_spmd.clone, body=%wide.region_34.37_spmd.clone.sunk | while | flops 2063563264 | bytes 196534736 | solution.py:122
  1111.5 32.9 %reduce-scatter.19.cloned.1.call-done = f32[96,192]{1,0:T(8,128)} async-done(((f32[768,192]{1,0:T(8,128)}), f32[96,192]{1,0:T(8,128)}) %reduce-scatter.19.cloned.1.call-update) | async-done | bytes 73744
  1146.1 68.3 %all-reduce.8.cloned.1.call-done = bf16[2048,768]{1,0:T(8,128)(2,1)} async-done(((bf16[2048,768]{1,0:T(8,128)(2,1)}), bf16[2048,768]{1,0:T(8,128)(2,1)}) %all-reduce.8.cloned.1.call-update) | async-done | bytes 3145744 | tf_op jit(solution)/shard_map/psum | solution.py:376
  1218.6 38.5 %all-reduce.2 = (f32[768]{0:T(1024)}, f32[768]{0:T(1024)}, f32[768,6]{0,1:T(8,128)}, f32[6,6]{0,1:T(8,128)S(1)}, f32[2,768,2]{1,2,0:T(2,128)}, /*index=5*/f32[2,768]{1,0:T(2,128)}, f32[6]{0:T(128)S(1)}) all-reduce(f32[768]{0:T(1024)S(1)} %get-tuple-element.226, ...), channel_id=1, replica_groups=mesh['dp'=4,'expert'=2,'tensor'=4] {'dp','expert'}, use_global_device_ids=true, to_apply=%region_40.42 | all-reduce | flops 10794 | bytes 86352 | tf_op jit(solution)/shard_map/psum | solution.py:389
  1267.0 18.9 %reduce-scatter.15.cloned.1.call-done = f32[96,576]{1,0:T(8,128)} async-done(((f32[768,576]{1,0:T(8,128)}), f32[96,576]{1,0:T(8,128)}) %reduce-scatter.15.cloned.1.call-update) | async-done | bytes 221200 | tf_op jit(solution)/shard_map/reduce_scatter | solution.py:386
  (430 shorter events, 596.7 us)
Async XLA Ops:
  7.2 270.5 %copy-start = (bf16[1,768,2,512]{3,2,1,0:T(2,128)(2,1)S(1)}, bf16[1,768,2,512]{3,2,1,0:T(2,128)(2,1)}, u32[]{:S(2)}) copy-start(bf16[1,768,2,512]{3,2,1,0:T(2,128)(2,1)} %param.34) | copy-start | bytes 4718596
  7.2 180.2 %all-reduce.6.cloned.1.call-start = ((), (), s32[]{:S(2)}) async-start(), calls=%async_computation.10 | async-start | bytes 6291456 | tf_op jit(solution)/shard_map/psum | solution.py:209
  16.0 97.3 %copy-start.35 = (bf16[192,768]{1,0:T(8,128)(2,1)S(1)}, bf16[192,768]{1,0:T(8,128)(2,1)}, u32[]{:S(2)}) copy-start(bf16[192,768]{1,0:T(8,128)(2,1)} %param.28) | copy-start | bytes 884740
  116.1 217.7 %reduce-scatter.11.cloned.1.call-start = ((), (), s32[]{:S(2)}) async-start(), calls=%async_computation.11 | async-start | bytes 3932160 | tf_op jit(solution)/shard_map/reduce_scatter | solution.py:246
  117.7 77.7 %copy-start.59 = (f32[768]{0:T(1024)}, f32[768]{0:T(1024)S(1)}, u32[]{:S(2)}) copy-start(f32[768]{0:T(1024)S(1)} %convert_element_type.125) | copy-start | bytes 9220
  124.5 91.1 %copy-start.70 = (s32[4096,1]{0,1:T(1,128)}, s32[4096,1]{0,1:T(1,128)S(1)}, u32[]{:S(2)}) copy-start(s32[4096,1]{0,1:T(1,128)S(1)} %compare_select_fusion) | copy-start | bytes 49156
  334.3 13.3 %all-to-all-start.1 = ((bf16[2,1024,192]{1,2,0:T(8,128)(2,1)}), bf16[2,1024,192]{1,2,0:T(8,128)(2,1)S(1)}, u32[]{:S(2)}, u32[]{:S(2)}) async-start(bf16[2,1024,192]{1,2,0:T(8,128)(2,1)} %reduce-scatter.11.cloned.1.call-done), calls=%async_computation.2 | async-start | bytes 1572864 | tf_op jit(solution)/shard_map/all_to_all | solution.py:249
  337.9 122.4 %all-gather.3.cloned.1.call-start = ((), (), s32[]{:S(2)}) async-start(), calls=%async_computation.12 | async-start | bytes 3932160 | tf_op jit(solution)/shard_map/all_gather | solution.py:250
  348.6 283.1 %reduce-scatter.13.cloned.1.call-start = ((), (), s32[]{:S(2)}) async-start(), calls=%async_computation.13 | async-start | bytes 3932160 | tf_op jit(solution)/shard_map/reduce_scatter | solution.py:246
  541.0 38.7 %copy-start.80 = (bf16[1,512,768]{2,1,0:T(8,128)(2,1)S(1)}, bf16[1,512,768]{2,1,0:T(8,128)(2,1)}, u32[]{:S(2)}) copy-start(bf16[1,512,768]{2,1,0:T(8,128)(2,1)} %param.35) | copy-start | bytes 2359300
  593.0 79.4 %copy-start.16 = (f32[2048,2]{1,0:T(8,128)S(1)}, f32[2048,2]{1,0:T(8,128)}, u32[]{:S(2)}) copy-start(f32[2048,2]{1,0:T(8,128)} %get-tuple-element.231) | copy-start | bytes 49156
  593.0 105.0 %all-gather.5.cloned.1.call-start = ((), (), s32[]{:S(2)}) async-start(), calls=%async_computation.14 | async-start | bytes 3932160 | tf_op jit(solution)/shard_map/all_gather | solution.py:250
  647.1 455.9 %reduce-scatter.21.cloned.1.call-start = ((), (), s32[]{:S(2)}) async-start(), calls=%async_computation.19 | async-start | bytes 983040
  687.0 418.8 %reduce-scatter.17.cloned.1.call-start = ((), (), s32[]{:S(2)}) async-start(), calls=%async_computation.17 | async-start | bytes 1966080 | tf_op jit(solution)/shard_map/reduce_scatter | solution.py:396
  697.9 446.5 %reduce-scatter.19.cloned.1.call-start = ((), (), s32[]{:S(2)}) async-start(), calls=%async_computation.18 | async-start | bytes 884736
  839.2 53.9 %copy-start.44 = (f32[2048,2,1]{0,2,1:T(1,128)}, f32[2048,2,1]{0,2,1:T(1,128)S(1)}, u32[]{:S(2)}) copy-start(f32[2048,2,1]{0,2,1:T(1,128)S(1)} %copy.102) | copy-start | bytes 49156
  840.8 52.3 %copy-start.46 = (f32[2048,2,1]{0,2,1:T(1,128)}, f32[2048,2,1]{0,2,1:T(1,128)S(1)}, u32[]{:S(2)}) copy-start(f32[2048,2,1]{0,2,1:T(1,128)S(1)} %copy.101) | copy-start | bytes 49156
  856.0 37.0 %copy-start.48 = (f32[2048,2]{0,1:T(2,128)}, f32[2048,2]{0,1:T(2,128)S(1)}, u32[]{:S(2)}) copy-start(f32[2048,2]{0,1:T(2,128)S(1)} %multiply_reduce_fusion.10) | copy-start | bytes 49156
  1085.4 129.0 %all-reduce.8.cloned.1.call-start = ((), (), s32[]{:S(2)}) async-start(), calls=%async_computation.15 | async-start | bytes 6291456 | tf_op jit(solution)/shard_map/psum | solution.py:376
  1091.7 194.1 %reduce-scatter.15.cloned.1.call-start = ((), (), s32[]{:S(2)}) async-start(), calls=%async_computation.16 | async-start | bytes 2211840 | tf_op jit(solution)/shard_map/reduce_scatter | solution.py:386
  1105.8 112.8 %copy-start.66 = (f32[2,768]{1,0:T(2,128)S(1)}, f32[2,768]{1,0:T(2,128)}, u32[]{:S(2)}) copy-start(f32[2,768]{1,0:T(2,128)} %get-tuple-element.219) | copy-start | bytes 18436
  1105.8 112.8 %copy-start.69 = (f32[768]{0:T(1024)S(1)}, f32[768]{0:T(1024)}, u32[]{:S(2)}) copy-start(f32[768]{0:T(1024)} %get-tuple-element.217) | copy-start | bytes 9220
  1105.8 112.9 %copy-start.74 = (f32[6]{0:T(128)S(1)}, f32[6]{0:T(128)}, u32[]{:S(2)}) copy-start(f32[6]{0:T(128)} %get-tuple-element.232) | copy-start | bytes 76
  1105.8 152.1 %copy-start.77 = (f32[6]{0:T(128)S(1)}, f32[6]{0:T(128)}, u32[]{:S(2)}) copy-start(f32[6]{0:T(128)} %copy-done.76) | copy-start | bytes 76
  (93 other events, 805.3 us)
Sparse Core Ops, SparseCore 0:
  116.2 71.1 all-reduce.5
  292.7 37.3 reduce-scatter.10
  348.7 28.3 all-gather.2
  593.1 38.4 reduce-scatter.12
  647.2 27.6 all-gather.4
  687.2 19.6 reduce-scatter.20
  709.1 34.5 reduce-scatter.16
  1085.5 58.8 reduce-scatter.18
  1146.9 67.3 all-reduce.7
  1218.7 67.1 reduce-scatter.14
where the time goes:
time: 1310 us; the launch traced here: 1290 us
  local copies, waits for them, and re-layouts  332 us (25%)
  other arithmetic  309 us (24%)
  matrix products  246 us (19%)
  waiting for transfers between devices  229 us (17%)
  blocking collectives  150 us (11%)
  between operations  17.2 us (1%)
    reduce_sum x1, other arithmetic, per_device(): grad_v_const = jnp.sum(const_mix[:, :, 1:2] * grad_const_out, axis=0)  81.5 us
    all_to_all x2, blocking collectives, send_out(): lax.all_to_all(buffer, 'expert', split_axis=0, concat_axis=0, tiled=True)  75.9 us
    psum x1, waiting for transfers between devices, per_device(): lax.psum(outer_cols(grad_qkv_rows, w_qkv).astype(jnp.bfloat16), 'tensor')  68.3 us
    psum x1, waiting for transfers between devices, per_device(): lax.psum(plain_dot(mixed_heads, w_out).astype(jnp.bfloat16), 'tensor')  62.9 us
    unnamed x163, local copies, waits for them, and re-layouts  42 us
    convert_element_type x4, other arithmetic, one_block(): grad_scores = (weights * (grad_weights - inner_total)).astype(jnp.bfloat16)  38.7 us
    reduce_scatter x2, waiting for transfers between devices, send_back(): lax.psum_scatter(shaped.astype(jnp.bfloat16), 'tensor', scatter_dimension...  38.6 us
    psum x1, blocking collectives, per_device(): lax.psum((grad_gain_attn, grad_gain_moe, grad_router, grad_prev_weight, g...  38.5 us
  transfers between devices with their start and end apart: 11, of which 6 were waited for; matrix products, arithmetic and copies ran while one was open for 47% of the time, Pallas kernels for 0%

commit v1 on v0

v1 whole, which is shorter than its diff:
```python
import functools

import jax
import jax.numpy as jnp
from jax import lax
from jax.experimental import pallas as pl
from jax.experimental.pallas import tpu as pltpu
from jax.sharding import PartitionSpec as P

HEAD_DIM = 64
EPSILON = 1e-06
AUX_WEIGHT = 0.01
SCORE_SCALE = 0.125
MAX_BLOCK = 256
LANES = 128
QB = 256
TB = 256
NEG = -1e30
F32 = jnp.float32
BF16 = jnp.bfloat16
VMEM_LIMIT = 48 * 1024 * 1024


def params(**more):
    return pltpu.CompilerParams(vmem_limit_bytes=VMEM_LIMIT, **more)


def nn(a, b):
    return lax.dot_general(a, b, (((1,), (0,)), ((), ())), preferred_element_type=F32)


def nt(a, b):
    return lax.dot_general(a, b, (((1,), (1,)), ((), ())), preferred_element_type=F32)


def tn(a, b):
    return lax.dot_general(a, b, (((0,), (0,)), ((), ())), preferred_element_type=F32)


def split_hi_lo(a):
    hi = a.astype(BF16)
    return hi, (a - hi.astype(F32)).astype(BF16)


def rms_factor(values):
    return lax.rsqrt(jnp.mean(values * values, axis=-1, keepdims=True) + EPSILON)


def swap(a, axis, bit):
    n = lax.axis_size(axis)
    return lax.ppermute(a, axis, [(i, i ^ bit) for i in range(n)])


def sum_over(a, axes):
    for axis in axes:
        bit = 1
        while bit < lax.axis_size(axis):
            a = a + swap(a, axis, bit)
            bit *= 2
    return a


def attn_fwd_kernel(heads, x_ref, gain_ref, wt_ref, bq_ref, bk_ref, h1_ref, qkvt_ref, ot_ref, lse_ref, kn_ref):
    tokens = x_ref.shape[0]
    win = min(2 * QB, tokens)

    def project(i, carry):
        rows = pl.ds(pl.multiple_of(i * TB, TB), TB)
        xb = x_ref[rows, :].astype(F32)
        h1 = (xb * rms_factor(xb) * gain_ref[...]).astype(BF16)
        h1_ref[rows, :] = h1
        qkvt = nt(wt_ref[...], h1)
        for h in range(heads):
            base = h * 3 * HEAD_DIM
            q = qkvt[base : base + HEAD_DIM].astype(BF16).astype(F32) * SCORE_SCALE
            k = qkvt[base + HEAD_DIM : base + 2 * HEAD_DIM].astype(BF16)
            v = qkvt[base + 2 * HEAD_DIM : base + 3 * HEAD_DIM].astype(BF16)
            qkvt_ref[base : base + HEAD_DIM, rows] = q.astype(BF16)
            qkvt_ref[base + HEAD_DIM : base + 2 * HEAD_DIM, rows] = k
            qkvt_ref[base + 2 * HEAD_DIM : base + 3 * HEAD_DIM, rows] = v
            kn_ref[h, rows, :] = k.astype(F32).T.astype(BF16)
        return carry

    lax.fori_loop(0, tokens // TB, project, 0)

    def query_block(i, carry):
        q0 = pl.multiple_of(i * QB, QB)
        w0 = pl.multiple_of(jnp.minimum(q0, tokens - win), QB)
        cols = pl.ds(q0, QB)
        allowed = bk_ref[pl.ds(w0, win), :] <= bq_ref[:, cols]
        state = []
        for h in range(heads):
            base = h * 3 * HEAD_DIM
            qt = qkvt_ref[base : base + HEAD_DIM, cols]
            s = nn(kn_ref[h, pl.ds(w0, win), :], qt)
            s = jnp.where(allowed, s, NEG)
            m = jnp.max(s, axis=0, keepdims=True)
            p = jnp.exp(s - m)
            total = jnp.sum(p, axis=0, keepdims=True)
            vt = qkvt_ref[base + 2 * HEAD_DIM : base + 3 * HEAD_DIM, pl.ds(w0, win)]
            acc = nn(vt, p.astype(BF16))
            state += [m, total, acc]

        def chunk(c, state):
            keys = pl.ds(pl.multiple_of(c * QB, QB), QB)
            new = []
            for h in range(heads):
                base = h * 3 * HEAD_DIM
                m, total, acc = state[3 * h : 3 * h + 3]
                qt = qkvt_ref[base : base + HEAD_DIM, cols]
                s = nn(kn_ref[h, keys, :], qt)
                m_new = jnp.maximum(m, jnp.max(s, axis=0, keepdims=True))
                p = jnp.exp(s - m_new)
                alpha = jnp.exp(m - m_new)
                total = total * alpha + jnp.sum(p, axis=0, keepdims=True)
                vt = qkvt_ref[base + 2 * HEAD_DIM : base + 3 * HEAD_DIM, keys]
                acc = acc * alpha + nn(vt, p.astype(BF16))
                new += [m_new, total, acc]
            return new

        state = lax.fori_loop(0, w0 // QB, chunk, state)
        for h in range(heads):
            m, total, acc = state[3 * h : 3 * h + 3]
            ot_ref[h * HEAD_DIM : (h + 1) * HEAD_DIM, cols] = (acc / total).astype(BF16)
            lse_ref[h : h + 1, cols] = m + jnp.log(total)
        return carry

    lax.fori_loop(0, tokens // QB, query_block, 0)


def attention_forward(x, gain, w_t, bq, bk, heads):
    tokens, width = x.shape
    cols = w_t.shape[0]
    lse_rows = -(-heads // 8) * 8
    return pl.pallas_call(
        functools.partial(attn_fwd_kernel, heads),
        name="attn_fwd",
        out_shape=(
            jax.ShapeDtypeStruct((tokens, width), BF16),
            jax.ShapeDtypeStruct((cols, tokens), BF16),
            jax.ShapeDtypeStruct((heads * HEAD_DIM, tokens), BF16),
            jax.ShapeDtypeStruct((lse_rows, tokens), F32),
        ),
        scratch_shapes=[pltpu.VMEM((heads, tokens, HEAD_DIM), BF16)],
        compiler_params=params(),
        cost_estimate=pl.CostEstimate(flops=20_000_000_000, bytes_accessed=12_000_000, transcendentals=9_000_000),
    )(x, gain, w_t, bq, bk)


def attn_bwd_kernel(heads, da_ref, wo_ref, qkvt_ref, ot_ref, lse_ref, bq_ref, bk_ref, dqkvt_ref, dot_ref, delta_ref, kn_ref, vn_ref, dk_ref, dv_ref):
    tokens = da_ref.shape[0]
    win = min(2 * QB, tokens)

    def project(i, carry):
        rows = pl.ds(pl.multiple_of(i * TB, TB), TB)
        dot = nt(wo_ref[...], da_ref[rows, :]).astype(BF16)
        dot_ref[:, rows] = dot
        prod = dot.astype(F32) * ot_ref[:, rows].astype(F32)
        for h in range(heads):
            base = h * 3 * HEAD_DIM
            delta_ref[h : h + 1, rows] = jnp.sum(prod[h * HEAD_DIM : (h + 1) * HEAD_DIM], axis=0, keepdims=True)
            kn_ref[h, rows, :] = qkvt_ref[base + HEAD_DIM : base + 2 * HEAD_DIM, rows].astype(F32).T.astype(BF16)
            vn_ref[h, rows, :] = qkvt_ref[base + 2 * HEAD_DIM : base + 3 * HEAD_DIM, rows].astype(F32).T.astype(BF16)
        return carry

    lax.fori_loop(0, tokens // TB, project, 0)
    dk_ref[...] = jnp.zeros_like(dk_ref)
    dv_ref[...] = jnp.zeros_like(dv_ref)

    def query_block(i, carry):
        q0 = pl.multiple_of(i * QB, QB)
        w0 = pl.multiple_of(jnp.minimum(q0, tokens - win), QB)
        cols = pl.ds(q0, QB)

        def tile(h, keys, allowed):
            base = h * 3 * HEAD_DIM
            qt = qkvt_ref[base : base + HEAD_DIM, cols]
            dot = dot_ref[h * HEAD_DIM : (h + 1) * HEAD_DIM, cols]
            s = nn(kn_ref[h, keys, :], qt)
            p = jnp.exp(s - lse_ref[h : h + 1, cols])
            if allowed is not None:
                p = jnp.where(allowed, p, 0.0)
            dp = nn(vn_ref[h, keys, :], dot)
            ds = (p * (dp - delta_ref[h : h + 1, cols])).astype(BF16)
            dv_ref[h, :, keys] += nt(dot, p.astype(BF16))
            dk_ref[h, :, keys] += nt(qt, ds)
            kt = qkvt_ref[base + HEAD_DIM : base + 2 * HEAD_DIM, keys]
            return nn(kt, ds)

        dq = []
        allowed = bk_ref[pl.ds(w0, win), :] <= bq_ref[:, cols]
        for h in range(heads):
            dq.append(tile(h, pl.ds(w0, win), allowed))

        def chunk(c, dq):
            keys = pl.ds(pl.multiple_of(c * QB, QB), QB)
            return [dq[h] + tile(h, keys, None) for h in range(heads)]

        dq = lax.fori_loop(0, w0 // QB, chunk, dq)
        for h in range(heads):
            base = h * 3 * HEAD_DIM
            dqkvt_ref[base : base + HEAD_DIM, cols] = (dq[h] * SCORE_SCALE).astype(BF16)
        return carry

    lax.fori_loop(0, tokens // QB, query_block, 0)
    for h in range(heads):
        base = h * 3 * HEAD_DIM
        dqkvt_ref[base + HEAD_DIM : base + 2 * HEAD_DIM, :] = dk_ref[h].astype(BF16)
        dqkvt_ref[base + 2 * HEAD_DIM : base + 3 * HEAD_DIM, :] = dv_ref[h].astype(BF16)


def attention_backward(da, w_out, qkvt, ot, lse, bq, bk, heads):
    tokens = da.shape[0]
    cols = qkvt.shape[0]
    return pl.pallas_call(
        functools.partial(attn_bwd_kernel, heads),
        name="attn_bwd",
        out_shape=jax.ShapeDtypeStruct((cols, tokens), BF16),
        scratch_shapes=[
            pltpu.VMEM((heads * HEAD_DIM, tokens), BF16),
            pltpu.VMEM((lse.shape[0], tokens), F32),
            pltpu.VMEM((heads, tokens, HEAD_DIM), BF16),
            pltpu.VMEM((heads, tokens, HEAD_DIM), BF16),
            pltpu.VMEM((heads, HEAD_DIM, tokens), F32),
            pltpu.VMEM((heads, HEAD_DIM, tokens), F32),
        ],
        compiler_params=params(),
        cost_estimate=pl.CostEstimate(flops=40_000_000_000, bytes_accessed=10_000_000, transcendentals=9_000_000),
    )(da, w_out, qkvt, ot, lse, bq, bk)


def lane_iota(rows):
    return lax.broadcasted_iota(jnp.int32, (rows, LANES), 1)


def column(values, lane, number):
    return jnp.sum(jnp.where(lane == number, values, 0.0), axis=1, keepdims=True)


def routing(logits, aux, types):
    lane = lane_iota(logits.shape[0])
    is_type = lane < types
    shown = jnp.where(is_type, logits, NEG)
    e = jnp.exp(shown - jnp.max(shown, axis=1, keepdims=True))
    probs = e / jnp.sum(e, axis=1, keepdims=True)
    aux = aux.astype(F32)
    first = column(aux, lane, types).astype(jnp.int32)
    second = column(aux, lane, types + 1).astype(jnp.int32)
    mask = jnp.where((lane == first) | (lane == second), 1.0, 0.0)
    return lane, probs, mask


def const_mix(logits, lane, types, c):
    l0 = column(logits, lane, types + 2 * c)
    l1 = column(logits, lane, types + 2 * c + 1)
    top = jnp.maximum(l0, l1)
    e0, e1 = jnp.exp(l0 - top), jnp.exp(l1 - top)
    total = e0 + e1
    return e0 / total, e1 / total


def post_attn_kernel(types, group, idx_ref, x_ref, *refs):
    ots, wos = refs[:group], refs[group : 2 * group]
    gain_ref, wcat_ref, aux_ref, wprev_ref = refs[2 * group : 2 * group + 4]
    x1_ref, h2_ref, lg_ref, ps_ref, wo_scr, ot_scr = refs[2 * group + 4 :]
    rows = ots[0].shape[0]
    me = idx_ref[0]

    @pl.when(pl.program_id(0) == 0)
    def _():
        for m in range(group):
            wo_scr[pl.ds(pl.multiple_of((me ^ m) * rows, HEAD_DIM), rows), :] = wos[m][...]
        ps_ref[...] = jnp.zeros_like(ps_ref)

    for m in range(group):
        ot_scr[pl.ds(pl.multiple_of((me ^ m) * rows, HEAD_DIM), rows), :] = ots[m][...]
    x1 = x_ref[...].astype(F32) + tn(ot_scr[...], wo_scr[...])
    x1_ref[...] = x1
    h2 = (x1 * rms_factor(x1) * gain_ref[...]).astype(BF16)
    h2_ref[...] = h2
    lg = nn(h2, wcat_ref[...]) + nn(aux_ref[...], wprev_ref[...])
    lg_ref[...] = lg
    _, probs, _ = routing(lg, aux_ref[...], types)
    ps_ref[0:1, :] += jnp.sum(probs, axis=0, keepdims=True)


def post_attention(me, x, ots, wos, gain, wcat, aux, wprev, types):
    tokens, width = x.shape
    rows = ots[0].shape[0]
    group = len(ots)
    block = lambda i, *_: (i, 0)
    fixed = lambda i, *_: (0, 0)
    grid_spec = pltpu.PrefetchScalarGridSpec(
        num_scalar_prefetch=1,
        grid=(tokens // TB,),
        in_specs=[pl.BlockSpec((TB, width), block)]
        + [pl.BlockSpec((rows, TB), lambda i, *_: (0, i))] * group
        + [pl.BlockSpec((rows, width), fixed)] * group
        + [
            pl.BlockSpec((1, width), fixed),
            pl.BlockSpec((width, LANES), fixed),
            pl.BlockSpec((TB, LANES), block),
            pl.BlockSpec((LANES, LANES), fixed),
        ],
        out_specs=[
            pl.BlockSpec((TB, width), block),
            pl.BlockSpec((TB, width), block),
            pl.BlockSpec((TB, LANES), block),
            pl.BlockSpec((8, LANES), fixed),
        ],
        scratch_shapes=[pltpu.VMEM((group * rows, width), BF16), pltpu.VMEM((group * rows, TB), BF16)],
    )
    return pl.pallas_call(
        functools.partial(post_attn_kernel, types, group),
        name="post_attn",
        grid_spec=grid_spec,
        out_shape=(
            jax.ShapeDtypeStruct((tokens, width), F32),
            jax.ShapeDtypeStruct((tokens, width), BF16),
            jax.ShapeDtypeStruct((tokens, LANES), F32),
            jax.ShapeDtypeStruct((8, LANES), F32),
        ),
        compiler_params=params(),
        cost_estimate=pl.CostEstimate(flops=3_000_000_000, bytes_accessed=20_000_000, transcendentals=300_000),
    )(me, x, *ots, *wos, gain, wcat, aux, wprev)


def expert_kernel(types, experts, halves, idx_ref, h2_ref, dy_ref, lg_ref, aux_ref, *refs):
    wgus, wds = refs[:experts], refs[experts : 2 * experts]
    eye_ref = refs[2 * experts]
    keep_ref, send_ref, gh_ref, du_ref, dlt_ref, acc_ref = refs[2 * experts + 1 :]
    me, half = idx_ref[0], idx_ref[1]
    hidden = wds[0].shape[0]
    h2, dy = h2_ref[...], dy_ref[...]
    lane, probs, mask = routing(lg_ref[...], aux_ref[...], types)
    gates = probs * mask
    dprobs = jnp.zeros_like(probs)
    for s in range(experts):
        e = me ^ s
        gate_col = column(gates, lane, e)
        u = nn(h2, wgus[s][...])
        dhr = nt(dy, wds[s][...])
        g, up = u[:, :hidden], u[:, hidden:]
        sig = 1.0 / (1.0 + jnp.exp(-g))
        silu = g * sig
        hid = silu * up
        gh_ref[e, :, :] = (hid * gate_col).astype(BF16)
        dg = jnp.sum(hid * dhr, axis=1, keepdims=True)
        dprobs = dprobs + jnp.where(lane == e, dg * mask, 0.0)
        dh = dhr * gate_col
        dgate = dh * up * sig * (1.0 + g * (1.0 - sig))
        dup = dh * silu
        du_ref[e, :, :hidden] = dgate.astype(BF16)
        du_ref[e, :, hidden:] = dup.astype(BF16)
        part = nt(du_ref[e, :, :], wgus[s][...])
        if s == 0:
            acc_ref[...] = part
        else:
            acc_ref[...] += part
    dlog = probs * (dprobs - jnp.sum(probs * dprobs, axis=1, keepdims=True))
    hi, lo = split_hi_lo(dlog)
    dlt_ref[...] = nt(eye_ref[...], hi) + nt(eye_ref[...], lo)
    half_cols = acc_ref.shape[1] // halves
    keep_ref[...] = acc_ref[:, pl.ds(pl.multiple_of(half * half_cols, LANES), half_cols)].astype(BF16)
    send_ref[...] = acc_ref[:, pl.ds(pl.multiple_of((1 - half) * half_cols, LANES), half_cols)].astype(BF16)


def experts_pass(idx, h2, dy, lg, aux, wgus, wds, eye, types):
    tokens, width = h2.shape
    experts = len(wgus)
    hidden = wds[0].shape[0]
    erows = eye.shape[0]
    block = lambda i, *_: (i, 0)
    fixed = lambda i, *_: (0, 0)
    grid_spec = pltpu.PrefetchScalarGridSpec(
        num_scalar_prefetch=1,
        grid=(tokens // TB,),
        in_specs=[
            pl.BlockSpec((TB, width), block),
            pl.BlockSpec((TB, width), block),
            pl.BlockSpec((TB, LANES), block),
            pl.BlockSpec((TB, LANES), block),
        ]
        + [pl.BlockSpec((width, 2 * hidden), fixed, pipeline_mode=pl.Buffered(1))] * experts
        + [pl.BlockSpec((hidden, width), fixed, pipeline_mode=pl.Buffered(1))] * experts
        + [pl.BlockSpec((erows, LANES), fixed)],
        out_specs=[
            pl.BlockSpec((TB, width // 2), block),
            pl.BlockSpec((TB, width // 2), block),
            pl.BlockSpec((experts, TB, hidden), lambda i, *_: (0, i, 0)),
            pl.BlockSpec((experts, TB, 2 * hidden), lambda i, *_: (0, i, 0)),
            pl.BlockSpec((erows, TB), lambda i, *_: (0, i)),
        ],
        scratch_shapes=[pltpu.VMEM((TB, width), F32)],
    )
    return pl.pallas_call(
        functools.partial(expert_kernel, types, experts, 2),
        name="experts",
        grid_spec=grid_spec,
        out_shape=(
            jax.ShapeDtypeStruct((tokens, width // 2), BF16),
            jax.ShapeDtypeStruct((tokens, width // 2), BF16),
            jax.ShapeDtypeStruct((experts, tokens, hidden), BF16),
            jax.ShapeDtypeStruct((experts, tokens, 2 * hidden), BF16),
            jax.ShapeDtypeStruct((erows, tokens), F32),
        ),
        compiler_params=params(),
        cost_estimate=pl.CostEstimate(flops=16_000_000_000, bytes_accessed=30_000_000, transcendentals=2_000_000),
    )(idx, h2, dy, lg, aux, *wgus, *wds, eye)


def down_kernel(experts, idx_ref, gh_ref, *refs):
    wds, (keep_ref, send_ref, acc_ref) = refs[:experts], refs[experts:]
    me, half = idx_ref[0], idx_ref[1]
    for s in range(experts):
        part = nn(gh_ref[me ^ s, :, :], wds[s][...])
        if s == 0:
            acc_ref[...] = part
        else:
            acc_ref[...] += part
    half_cols = keep_ref.shape[1]
    keep_ref[...] = acc_ref[:, pl.ds(pl.multiple_of(half * half_cols, LANES), half_cols)].astype(BF16)
    send_ref[...] = acc_ref[:, pl.ds(pl.multiple_of((1 - half) * half_cols, LANES), half_cols)].astype(BF16)


def down_pass(idx, gh, wds):
    experts, tokens, hidden = gh.shape
    width = wds[0].shape[1]
    block = lambda i, *_: (i, 0)
    fixed = lambda i, *_: (0, 0)
    grid_spec = pltpu.PrefetchScalarGridSpec(
        num_scalar_prefetch=1,
        grid=(tokens // TB,),
        in_specs=[pl.BlockSpec((experts, TB, hidden), lambda i, *_: (0, i, 0))]
        + [pl.BlockSpec((hidden, width), fixed, pipeline_mode=pl.Buffered(1))] * experts,
        out_specs=[pl.BlockSpec((TB, width // 2), block)] * 2,
        scratch_shapes=[pltpu.VMEM((TB, width), F32)],
    )
    return pl.pallas_call(
        functools.partial(down_kernel, experts),
        name="down",
        grid_spec=grid_spec,
        out_shape=(jax.ShapeDtypeStruct((tokens, width // 2), BF16),) * 2,
        compiler_params=params(),
        cost_estimate=pl.CostEstimate(flops=3_500_000_000, bytes_accessed=9_000_000, transcendentals=0),
    )(idx, gh, *wds)


def middle_kernel(types, ffn, total_tokens, idx_ref, mine_ref, theirs_ref, x1_ref, dy_ref, lg_ref, aux_ref, dlt_ref, eye_ref, count_ref, gain_ref, wcat_ref, vt_ref, wprevt_ref, dx1_ref, da_ref, gp_ref, g1_ref, g2_ref, g3_ref, g4_ref, scr_ref):
    half = idx_ref[1]
    half_cols = mine_ref.shape[1]
    scr_ref[:, pl.ds(pl.multiple_of(half * half_cols, LANES), half_cols)] = mine_ref[...]
    scr_ref[:, pl.ds(pl.multiple_of((1 - half) * half_cols, LANES), half_cols)] = theirs_ref[...]
    first = pl.program_id(0) == 0

    @pl.when(first)
    def _():
        for ref in (g1_ref, g2_ref, g3_ref, g4_ref):
            ref[...] = jnp.zeros_like(ref)

    gain = gain_ref[...]
    x1 = x1_ref[...]
    r2 = rms_factor(x1)
    n2 = x1 * r2
    h2 = (n2 * gain).astype(BF16)
    dyb = dy_ref[...]
    dy = dyb.astype(F32)
    lg = lg_ref[...]
    lane, probs, mask = routing(lg, aux_ref[...], types)
    gates = probs * mask
    a = jnp.sum(dy * h2.astype(F32), axis=1, keepdims=True)
    b = nn(dyb, vt_ref[...])
    coef = column(gates, lane, ffn + 1)
    dprobs = jnp.where(lane == ffn + 1, a, 0.0)
    dlc = jnp.zeros_like(probs)
    vcoef = jnp.zeros_like(probs)
    for c in range(2):
        m0, m1 = const_mix(lg, lane, types, c)
        g = column(gates, lane, ffn + 2 + c)
        bc = column(b, lane, c)
        dprobs = dprobs + jnp.where(lane == ffn + 2 + c, m0 * a + m1 * bc, 0.0)
        dm0, dm1 = g * a, g * bc
        inner = m0 * dm0 + m1 * dm1
        dlc = dlc + jnp.where(lane == types + 2 * c, m0 * (dm0 - inner), 0.0)
        dlc = dlc + jnp.where(lane == types + 2 * c + 1, m1 * (dm1 - inner), 0.0)
        coef = coef + g * m0
        vcoef = vcoef + jnp.where(lane == c, g * m1, 0.0)
    dprobs = dprobs * mask + count_ref[...] * (AUX_WEIGHT * types / (2.0 * total_tokens * total_tokens))
    dlog = probs * (dprobs - jnp.sum(probs * dprobs, axis=1, keepdims=True))
    hi, lo = split_hi_lo(dlt_ref[...])
    dl = dlog + dlc + tn(hi, eye_ref[...]) + tn(lo, eye_ref[...])
    dhi, dlo = split_hi_lo(dl)
    dh2 = scr_ref[...].astype(F32) + coef * dy + nt(dhi, wcat_ref[...]) + nt(dlo, wcat_ref[...])
    dn2 = dh2 * gain
    dx1 = dy + r2 * (dn2 - n2 * jnp.mean(dn2 * n2, axis=1, keepdims=True))
    dx1_ref[...] = dx1
    da_ref[...] = dx1.astype(BF16)
    gp_ref[...] = nn(dhi, wprevt_ref[...]) + nn(dlo, wprevt_ref[...])
    g1_ref[...] += tn(dhi, h2) + tn(dlo, h2)
    vhi, vlo = split_hi_lo(vcoef)
    g2_ref[...] += tn(vhi, dyb) + tn(vlo, dyb)
    g3_ref[0:1, :] += jnp.sum(dh2 * n2, axis=0, keepdims=True)
    g4_ref[...] += tn(aux_ref[...], dhi) + tn(aux_ref[...], dlo)


def middle_pass(idx, mine, theirs, x1, dy, lg, aux, dlt, eye, count, gain, wcat, vt, wprevt, types, ffn, total_tokens):
    tokens, width = x1.shape
    erows = dlt.shape[0]
    block = lambda i, *_: (i, 0)
    fixed = lambda i, *_: (0, 0)
    grid_spec = pltpu.PrefetchScalarGridSpec(
        num_scalar_prefetch=1,
        grid=(tokens // TB,),
        in_specs=[
            pl.BlockSpec((TB, width // 2), block),
            pl.BlockSpec((TB, width // 2), block),
            pl.BlockSpec((TB, width), block),
            pl.BlockSpec((TB, width), block),
            pl.BlockSpec((TB, LANES), block),
            pl.BlockSpec((TB, LANES), block),
            pl.BlockSpec((erows, TB), lambda i, *_: (0, i)),
            pl.BlockSpec((erows, LANES), fixed),
            pl.BlockSpec((1, LANES), fixed),
            pl.BlockSpec((1, width), fixed),
            pl.BlockSpec((width, LANES), fixed),
            pl.BlockSpec((width, LANES), fixed),
            pl.BlockSpec((LANES, LANES), fixed),
        ],
        out_specs=[
            pl.BlockSpec((TB, width), block),
            pl.BlockSpec((TB, width), block),
            pl.BlockSpec((TB, LANES), block),
            pl.BlockSpec((LANES, width), fixed),
            pl.BlockSpec((LANES, width), fixed),
            pl.BlockSpec((8, width), fixed),
            pl.BlockSpec((LANES, LANES), fixed),
        ],
        scratch_shapes=[pltpu.VMEM((TB, width), BF16)],
    )
    return pl.pallas_call(
        functools.partial(middle_kernel, types, ffn, total_tokens),
        name="middle",
        grid_spec=grid_spec,
        out_shape=(
            jax.ShapeDtypeStruct((tokens, width), F32),
            jax.ShapeDtypeStruct((tokens, width), BF16),
            jax.ShapeDtypeStruct((tokens, LANES), F32),
            jax.ShapeDtypeStruct((LANES, width), F32),
            jax.ShapeDtypeStruct((LANES, width), F32),
            jax.ShapeDtypeStruct((8, width), F32),
            jax.ShapeDtypeStruct((LANES, LANES), F32),
        ),
        compiler_params=params(),
        cost_estimate=pl.CostEstimate(flops=4_000_000_000, bytes_accessed=25_000_000, transcendentals=300_000),
    )(idx, mine, theirs, x1, dy, lg, aux, dlt, eye, count, gain, wcat, vt, wprevt)


def output_kernel(types, ffn, idx_ref, mine_ref, theirs_ref, x1_ref, h2_ref, lg_ref, aux_ref, v_ref, out_ref, scr_ref):
    half = idx_ref[1]
    half_cols = mine_ref.shape[1]
    scr_ref[:, pl.ds(pl.multiple_of(half * half_cols, LANES), half_cols)] = mine_ref[...]
    scr_ref[:, pl.ds(pl.multiple_of((1 - half) * half_cols, LANES), half_cols)] = theirs_ref[...]
    lg = lg_ref[...]
    lane, probs, mask = routing(lg, aux_ref[...], types)
    gates = probs * mask
    coef = column(gates, lane, ffn + 1)
    out = x1_ref[...] + scr_ref[...].astype(F32)
    for c in range(2):
        m0, m1 = const_mix(lg, lane, types, c)
        g = column(gates, lane, ffn + 2 + c)
        coef = coef + g * m0
        out = out + (g * m1) * v_ref[c : c + 1, :]
    out_ref[...] = out + coef * h2_ref[...].astype(F32)


def output_pass(idx, mine, theirs, x1, h2, lg, aux, v, types, ffn):
    tokens, width = x1.shape
    block = lambda i, *_: (i, 0)
    fixed = lambda i, *_: (0, 0)
    grid_spec = pltpu.PrefetchScalarGridSpec(
        num_scalar_prefetch=1,
        grid=(tokens // TB,),
        in_specs=[
            pl.BlockSpec((TB, width // 2), block),
            pl.BlockSpec((TB, width // 2), block),
            pl.BlockSpec((TB, width), block),
            pl.BlockSpec((TB, width), block),
            pl.BlockSpec((TB, LANES), block),
            pl.BlockSpec((TB, LANES), block),
            pl.BlockSpec((8, width), fixed),
        ],
        out_specs=pl.BlockSpec((TB, width), block),
        scratch_shapes=[pltpu.VMEM((TB, width), BF16)],
    )
    return pl.pallas_call(
        functools.partial(output_kernel, types, ffn),
        name="output",
        grid_spec=grid_spec,
        out_shape=jax.ShapeDtypeStruct((tokens, width), F32),
        compiler_params=params(),
        cost_estimate=pl.CostEstimate(flops=20_000_000, bytes_accessed=22_000_000, transcendentals=300_000),
    )(idx, mine, theirs, x1, h2, lg, aux, v)


def last_kernel(idx_ref, mine_ref, theirs_ref, x_ref, dx1_ref, gain_ref, out_ref, scr_ref):
    half = idx_ref[1]
    half_cols = mine_ref.shape[1]
    scr_ref[:, pl.ds(pl.multiple_of(half * half_cols, LANES), half_cols)] = mine_ref[...]
    scr_ref[:, pl.ds(pl.multiple_of((1 - half) * half_cols, LANES), half_cols)] = theirs_ref[...]
    x = x_ref[...].astype(F32)
    r1 = rms_factor(x)
    n1 = x * r1
    dn1 = scr_ref[...].astype(F32) * gain_ref[...]
    out_ref[...] = dx1_ref[...] + r1 * (dn1 - n1 * jnp.mean(dn1 * n1, axis=1, keepdims=True))


def last_pass(idx, mine, theirs, x, dx1, gain):
    tokens, width = x.shape
    block = lambda i, *_: (i, 0)
    fixed = lambda i, *_: (0, 0)
    grid_spec = pltpu.PrefetchScalarGridSpec(
        num_scalar_prefetch=1,
        grid=(tokens // TB,),
        in_specs=[
            pl.BlockSpec((TB, width // 2), block),
            pl.BlockSpec((TB, width // 2), block),
            pl.BlockSpec((TB, width), block),
            pl.BlockSpec((TB, width), block),
            pl.BlockSpec((1, width), fixed),
        ],
        out_specs=pl.BlockSpec((TB, width), block),
        scratch_shapes=[pltpu.VMEM((TB, width), BF16)],
    )
    return pl.pallas_call(
        last_kernel,
        name="last",
        grid_spec=grid_spec,
        out_shape=jax.ShapeDtypeStruct((tokens, width), F32),
        compiler_params=params(),
        cost_estimate=pl.CostEstimate(flops=20_000_000, bytes_accessed=20_000_000, transcendentals=2_000),
    )(idx, mine, theirs, x, dx1, gain)


def group_sum(keep, send):
    part = (keep.astype(F32) + swap(send, "tensor", 1).astype(F32)).astype(BF16)
    bit = 2
    while bit < lax.axis_size("tensor"):
        part = (part.astype(F32) + swap(part, "tensor", bit).astype(F32)).astype(BF16)
        bit *= 2
    return part, swap(part, "tensor", 1)


def gather_group(a):
    out = [a]
    bit = lax.axis_size("tensor") // 2
    parts = {0: a}
    while bit:
        parts.update({m | bit: swap(p, "tensor", bit) for m, p in list(parts.items())})
        bit //= 2
    return [parts[m] for m in range(len(parts))]


def per_device(hidden_in, prev_logits, routes, block_ids, cotangent, gain_attn, w_qkv, w_out, gain_moe, w_router, w_prev, w_const, v_const, w_gate_up, w_down):
    tokens, width = hidden_in.shape
    types = w_router.shape[1]
    experts = lax.axis_size("expert")
    heads = w_out.shape[0] // HEAD_DIM
    hidden = w_down.shape[1]
    total_tokens = tokens * lax.axis_size(("dp", "expert"))
    t_index, x_index = lax.axis_index("tensor"), lax.axis_index("expert")
    t_idx = jnp.stack([t_index, t_index % 2]).astype(jnp.int32)
    x_idx = jnp.stack([x_index, t_index % 2]).astype(jnp.int32)

    wgu, wd = w_gate_up[0].reshape(width, 2 * hidden), w_down[0]
    wgus = [wgu] + [swap(wgu, "expert", s) for s in range(1, experts)]
    wds = [wd] + [swap(wd, "expert", s) for s in range(1, experts)]
    wos = gather_group(w_out)
    gain_first = gain_attn.astype(F32)[None]
    gain_second = gain_moe.astype(F32)[None]
    consts = w_const.transpose(1, 0, 2).reshape(width, 4)
    wcat = jnp.pad(jnp.concatenate([w_router, consts], axis=1), ((0, 0), (0, LANES - types - 4)))
    aux = jnp.concatenate([prev_logits, routes.astype(BF16)], axis=1)
    aux = jnp.pad(aux, ((0, 0), (0, LANES - types - 2)))
    wprev = jnp.pad(w_prev, ((0, LANES - types), (0, LANES - types)))
    wprevt = jnp.pad(w_prev.T, ((0, LANES - types), (0, LANES - types)))
    vt = jnp.pad(v_const.T, ((0, 0), (0, LANES - 2)))
    vrows = jnp.pad(v_const.astype(F32), ((0, 6), (0, 0)))
    erows = -(-types // 16) * 16
    eye = jnp.eye(erows, LANES, dtype=BF16)
    lanes = jnp.arange(LANES, dtype=jnp.int32)
    chosen = (routes[:, :, None] == lanes[None, None, :]).astype(F32)
    count = sum_over(jnp.sum(chosen, axis=(0, 1))[None], ("expert", "dp"))
    bq, bk = block_ids, block_ids.reshape(tokens, 1)

    h1, qkvt, ot, lse = attention_forward(hidden_in, gain_first, w_qkv.T, bq, bk, heads)
    ots = gather_group(ot)
    x1, h2, lg, prob_part = post_attention(t_idx, hidden_in, ots, wos, gain_second, wcat, aux, wprev, types)
    keep, send, gh, du, dlt = experts_pass(x_idx, h2, cotangent, lg, aux, wgus, wds, eye, types)
    mine, theirs = group_sum(keep, send)
    dlt = sum_over(dlt, ("tensor",))
    fkeep, fsend = down_pass(x_idx, gh, wds)
    grad_gate_up = jnp.einsum("td,etf->edf", h2, du, preferred_element_type=F32).astype(BF16)
    grad_down = jnp.einsum("td,etf->edf", cotangent, gh, preferred_element_type=F32).astype(BF16)
    fmine, ftheirs = group_sum(fkeep, fsend)
    dx1, da, gp, g1, g2, g3, g4 = middle_pass(
        x_idx, mine, theirs, x1, cotangent, lg, aux, dlt, eye, count, gain_second, wcat, vt, wprevt, types, experts, total_tokens
    )
    srows = -(-(types + 4) // 8) * 8
    prow = -(-types // 8) * 8
    small = jnp.concatenate(
        [
            g1[:srows],
            g2[:8],
            g3,
            jnp.pad(g4[:prow], ((0, 0), (0, width - LANES))),
            jnp.pad(prob_part, ((0, 0), (0, width - LANES))),
        ],
        axis=0,
    )
    small = sum_over(small, ("expert", "dp"))
    grad_out = lax.dot_general(ot, da, (((1,), (0,)), ((), ())), preferred_element_type=F32)
    dqkvt = attention_backward(da, w_out, qkvt, ot, lse, bq, bk, heads)
    output = output_pass(x_idx, fmine, ftheirs, x1, h2, lg, aux, vrows, types, experts)

    dh1 = lax.dot_general(dqkvt, w_qkv, (((0,), (1,)), ((), ())), preferred_element_type=F32).astype(BF16)
    core = t_index % 2
    half_cols = width // 2
    last_mine, last_theirs = group_sum(
        lax.dynamic_slice_in_dim(dh1, core * half_cols, half_cols, 1),
        lax.dynamic_slice_in_dim(dh1, (1 - core) * half_cols, half_cols, 1),
    )
    grad_qkv = lax.dot_general(h1, dqkvt, (((0,), (1,)), ((), ())), preferred_element_type=F32)
    gain_part = jnp.sum(grad_qkv * w_qkv.astype(F32), axis=1)
    grad_gain = sum_over(gain_part[None], ("tensor", "expert", "dp"))[0] / gain_first[0]
    grad_input = last_pass(x_idx, last_mine, last_theirs, hidden_in, dx1, gain_first)

    grad_gate_up = lax.psum_scatter(grad_gate_up, "expert", scatter_dimension=0, tiled=True)
    grad_gate_up = lax.psum_scatter(grad_gate_up, "dp", scatter_dimension=1, tiled=True).astype(F32)
    grad_down = lax.psum_scatter(grad_down, "expert", scatter_dimension=0, tiled=True)
    grad_down = lax.psum_scatter(grad_down, "dp", scatter_dimension=1, tiled=True).astype(F32)
    grad_qkv = lax.psum_scatter(grad_qkv, ("dp", "expert"), scatter_dimension=0, tiled=True)
    grad_out = lax.psum_scatter(grad_out, ("dp", "expert"), scatter_dimension=1, tiled=True)

    prob_all = small[srows + 16 + prow, :types]
    count_all = count[0, :types]
    balance_loss = types * jnp.sum((count_all / (2.0 * total_tokens)) * prob_all / total_tokens)
    load = jnp.stack([count_all / (2.0 * tokens), prob_all / tokens])
    return (
        output,
        grad_input,
        gp[:, :types],
        grad_gain,
        grad_qkv,
        grad_out,
        small[srows + 8],
        small[:types].T,
        small[srows + 16 : srows + 16 + types, :types],
        small[types : types + 4].reshape(2, 2, width).transpose(0, 2, 1),
        small[srows : srows + 2],
        grad_gate_up.reshape(1, -1, 2, hidden),
        grad_down.transpose(0, 2, 1),
        balance_loss,
        load,
    )


def solution(mesh):
    tok = P(("dp", "expert"), None)
    return jax.shard_map(
        per_device,
        mesh=mesh,
        in_specs=(
            tok,
            tok,
            tok,
            tok,
            tok,
            P(),
            P(None, "tensor"),
            P("tensor", None),
            P(),
            P(),
            P(),
            P(),
            P(),
            P("expert", None, None, "tensor"),
            P("expert", "tensor", None),
        ),
        out_specs=(
            tok,
            tok,
            tok,
            P(),
            P(("dp", "expert"), "tensor"),
            P("tensor", ("dp", "expert")),
            P(),
            P(),
            P(),
            P(),
            P(),
            P("expert", "dp", None, "tensor"),
            P("expert", "tensor", "dp"),
            P(),
            P(),
        ),
        check_vma=False,
    )
```

time: 1310 us -> 457 us (0.35); the launches traced: 1290 us -> 455 us
  other arithmetic: 309 us -> 16.3 us
  local copies, waits for them, and re-layouts: 332 us -> 57.4 us
  matrix products: 246 us -> 30.5 us
  Pallas kernels: 0 us -> 171 us
  blocking collectives: 150 us -> 0 us
  waiting for transfers between devices: 229 us -> 135 us
  starting transfers between devices: 4.58 us -> 27.1 us
    dot_general x47 -> x4, matrix products: 238 us -> 26 us  [the longest x1 11.4 us: per_device(): jnp.einsum('td,etf->edf', h2, du, preferred_element_type=F32).astype(BF16)]
    reduce_sum x16 -> x1, other arithmetic: 185 us -> 0.85 us  [per_device(): count = sum_over(jnp.sum(chosen, axis=(0, 1))[None], ('expert', 'dp'))]
    pallas_call x0 -> x8, Pallas kernels: none -> 171 us  [the longest x1 44.3 us: attention_forward(): pl.pallas_call(functools.partial(attn_fwd_kernel, heads), name='attn_fwd'...]
    ppermute x0 -> x30, waiting for transfers between devices: none -> 135 us  [swap(): return lax.ppermute(a, axis, [(i, i ^ bit) for i in range(n)])]
    psum x2 -> x0, waiting for transfers between devices: 131 us -> none  [the longest x1 68.3 us: per_device(): lax.psum(outer_cols(grad_qkv_rows, w_qkv).astype(jnp.bfloat16), 'tensor')]
    mul x18 -> x0, local copies, waits for them, and re-layouts: 121 us -> none  [the longest x4 31.1 us: per_device(): route_values = ffn_values + copy_mask[..., None] * moe_values[:, None, :]]
    all_to_all x3 -> x0, blocking collectives: 91.4 us -> none  [the longest x2 75.9 us: send_out(): lax.all_to_all(buffer, 'expert', split_axis=0, concat_axis=0, tiled=True)]
    psum x2 -> x0, blocking collectives: 58.7 us -> none  [the longest x1 38.5 us: per_device(): lax.psum((grad_gain_attn, grad_gain_moe, grad_router, grad_prev_weight, g...]
  transfers between devices with their start and end apart: 11 -> 36, of which waited for: 6 -> 13; matrix products, arithmetic and copies ran while one was open for 47% -> 19% of each run, Pallas kernels for 0% -> 22%
where the time goes in v1:
time: 457 us; the launch traced here: 455 us
  Pallas kernels  171 us (37%)
  waiting for transfers between devices  135 us (30%)
  local copies, waits for them, and re-layouts  57.4 us (13%)
  matrix products  30.5 us (7%)
  starting transfers between devices  27.1 us (6%)
  between operations  16.5 us (4%)
  other arithmetic  16.3 us (4%)
    ppermute x30, waiting for transfers between devices, swap(): return lax.ppermute(a, axis, [(i, i ^ bit) for i in range(n)])  135 us
    unnamed x94, local copies, waits for them, and re-layouts  47 us
    pallas_call x1, Pallas kernels, attention_forward(): pl.pallas_call(functools.partial(attn_fwd_kernel, heads), name='attn_fwd'...  44.3 us
    pallas_call x1, Pallas kernels, attention_backward(): pl.pallas_call(functools.partial(attn_bwd_kernel, heads), name='attn_bwd'...  40.3 us
    pallas_call x1, Pallas kernels, experts_pass(): pl.pallas_call(functools.partial(expert_kernel, types, experts, 2), name=...  27.1 us
    ppermute x30, starting transfers between devices, swap(): return lax.ppermute(a, axis, [(i, i ^ bit) for i in range(n)])  26.5 us
    pallas_call x1, Pallas kernels, middle_pass(): pl.pallas_call(functools.partial(middle_kernel, types, ffn, total_tokens)...  15.9 us
    pallas_call x1, Pallas kernels, post_attention(): pl.pallas_call(functools.partial(post_attn_kernel, types, group), name='p...  12.7 us
  transfers between devices with their start and end apart: 36, of which 13 were waited for; matrix products, arithmetic and copies ran while one was open for 19% of the time, Pallas kernels for 22%

profile of v1, /device:TPU:0, one launch (start us, length us, event | category | flops | bytes accessed | tf_op | source)
XLA Modules:
  0.0 454.5 jit_solution(4230744967279113282)
XLA Ops:
  10.9 44.3 %attn_fwd.1 = (bf16[2048,768]{1,0:T(8,128)(2,1)}, bf16[576,2048]{1,0:T(8,128)(2,1)S(1)}, bf16[192,2048]{1,0:T(8,128)(2,1)}, f32[8,2048]{1,0:T(8,128)S(1)}) custom-call(bf16[2048,768]{1,0:T(8,128)(2,1)} %x_ref.5, f32[1,768]{1,0:T(1,128)S(1)} %broadcast_in_dim.16.gain_ref, bf16[576,768]{1,0:T(8,128)(2,1)S(1)} %bitcast.68, s32[1,2048]{1,0:T(1,128)S(1)} %copy-done.7, ...), custom_call_target="tpu_custom_call" | custom-call | flops 20000000000 | bytes 12000000 | tf_op jit(solution)/shard_map/attn_fwd/pallas_call | solution.py:135
  61.9 15.0 %collective-permute-done.1.refs_2_ = bf16[192,2048]{1,0:T(8,128)(2,1)S(1)} collective-permute-done((bf16[192,2048]{1,0:T(8,128)(2,1)}, bf16[192,2048]{1,0:T(8,128)(2,1)S(1)}, u32[]{:S(2)}, u32[]{:S(2)}) %collective-permute-start.1) | collective-permute-done | bytes 786464 | tf_op jit(solution)/shard_map/ppermute | solution.py:51
  77.7 4.6 %collective-permute-done.4.refs_6_ = bf16[192,768]{1,0:T(8,128)(2,1)S(1)} collective-permute-done((bf16[192,768]{1,0:T(8,128)(2,1)S(1)}, bf16[192,768]{1,0:T(8,128)(2,1)S(1)}, u32[]{:S(2)}, u32[]{:S(2)}) %collective-permute-start.4) | collective-permute-done | bytes 294944 | tf_op jit(solution)/shard_map/ppermute | solution.py:51
  89.1 12.7 %post_attn.1 = (f32[2048,768]{1,0:T(8,128)}, bf16[2048,768]{1,0:T(8,128)(2,1)}, f32[2048,128]{1,0:T(8,128)S(1)}, f32[8,128]{1,0:T(8,128)S(1)}) custom-call(s32[2]{0:T(128)S(1)} %pad_add_fusion.1.idx_ref, bf16[2048,768]{1,0:T(8,128)(2,1)} %x_ref.5, bf16[192,2048]{1,0:T(8,128)(2,1)} %get-tuple-element.37.refs_0_.ot_ref, ...), custom_call_target="tpu_custom_call" | custom-call | flops 3000000000 | bytes 20000000 | tf_op jit(solution)/shard_map/post_attn/pallas_call | solution.py:313
  101.7 11.1 %collective-permute-done.7.refs_3_.refs_1_ = bf16[512,768]{1,0:T(8,128)(2,1)} collective-permute-done((bf16[512,768]{1,0:T(8,128)(2,1)S(1)}, bf16[512,768]{1,0:T(8,128)(2,1)}, u32[]{:S(2)}, u32[]{:S(2)}) %collective-permute-start.7) | collective-permute-done | bytes 786464 | tf_op jit(solution)/shard_map/ppermute | solution.py:51
  112.9 27.1 %experts.1 = (bf16[2048,384]{1,0:T(8,128)(2,1)S(1)}, bf16[2048,384]{1,0:T(8,128)(2,1)}, bf16[2,2048,512]{2,1,0:T(8,128)(2,1)}, bf16[2,2048,1024]{2,1,0:T(8,128)(2,1)}, f32[16,2048]{1,0:T(8,128)S(1)}) custom-call(s32[2]{0:T(128)S(1)} %pad_add_fusion.idx_ref, bf16[2048,768]{1,0:T(8,128)(2,1)} %get-tuple-element.38.h2_ref, bf16[2048,768]{1,0:T(8,128)(2,1)} %dy_ref.3, ...), custom_call_target="tpu_custom_call" | custom-call | flops 16000000000 | bytes 30000000 | tf_op jit(solution)/shard_map/experts/pallas_call | solution.py:396
  140.0 6.9 %fusion.9 = bf16[2,768,512]{1,2,0:T(8,128)(2,1)} fusion(bf16[2,2048,512]{2,1,0:T(8,128)(2,1)} %get-tuple-element.40.gh_ref, bf16[2048,768]{1,0:T(8,128)(2,1)S(1)} %copy-done.36), kind=kOutput, calls=%fused_computation.17 | convolution fusion | flops 3222011904 | bytes 8912896 | tf_op jit(solution)/shard_map/td,etf->edf/dot_general | solution.py:703
  147.1 11.4 %convert_bitcast_fusion = bf16[2,768,1024]{1,2,0:T(8,128)(2,1)} fusion(bf16[2,2048,1024]{2,1,0:T(8,128)(2,1)} %get-tuple-element.58, bf16[2048,768]{1,0:T(8,128)(2,1)} %get-tuple-element.38.h2_ref), kind=kOutput, calls=%fused_computation.5 | convolution fusion | flops 6444023808 | bytes 14680064 | tf_op jit(solution)/shard_map/td,etf->edf/dot_general | solution.py:702
  158.6 3.6 collective-permute-done.11
  163.0 36.1 %collective-permute-done.12 = bf16[2048,384]{1,0:T(8,128)(2,1)S(1)} collective-permute-done((bf16[2048,384]{1,0:T(8,128)(2,1)S(1)}, bf16[2048,384]{1,0:T(8,128)(2,1)S(1)}, u32[]{:S(2)}, u32[]{:S(2)}) %collective-permute-start.12) | collective-permute-done | bytes 1572896 | tf_op jit(solution)/shard_map/ppermute | solution.py:51
  199.7 4.8 %copy.91 = bf16[1,768,512]{2,0,1:T(2,128)(2,1)} copy(bf16[1,768,512]{1,2,0:T(8,128)(2,1)} %reduce-scatter.17.cloned.1.call-done) | data formatting | bytes 1572864
  221.2 15.9 %middle.1 = (f32[2048,768]{1,0:T(8,128)}, bf16[2048,768]{1,0:T(8,128)(2,1)}, f32[2048,128]{1,0:T(8,128)S(1)}, f32[128,768]{1,0:T(8,128)S(1)}, f32[128,768]{1,0:T...) custom-call(s32[2]{0:T(128)S(1)} %pad_add_fusion.idx_ref, bf16[2048,384]{1,0:T(8,128)(2,1)S(1)} %add_convert_fusion.2.mine_ref, ...), custom_call_target="tpu_custom_call" | custom-call | flops 4000000000 | bytes 25000000 | tf_op jit(solution)/shard_map/middle/pallas_call | solution.py:540
  240.2 4.4 convolution_bitcast_fusion
  244.8 9.2 %down.1 = (bf16[2048,384]{1,0:T(8,128)(2,1)S(1)}, bf16[2048,384]{1,0:T(8,128)(2,1)}) custom-call(s32[2]{0:T(128)S(1)} %pad_add_fusion.idx_ref, bf16[2,2048,512]{2,1,0:T(8,128)(2,1)} %get-tuple-element.40.gh_ref, bf16[512,768]{1,0:T(8,128)(2,1)S(1)} %bitcast.71, bf16[512,768]{1,0:T(8,128)(2,1)} %collective-permute-done.7.refs_3_.refs_1_), custom_call_target="tpu_custom_call" | custom-call | flops 3500000000 | bytes 9000000 | tf_op jit(solution)/shard_map/down/pallas_call | solution.py:439
  253.9 8.4 %copy.89 = bf16[1,768,1024]{2,0,1:T(2,128)(2,1)} copy(bf16[1,768,1024]{1,2,0:T(8,128)(2,1)} %reduce-scatter.15.cloned.1.call-done) | data formatting | bytes 3145728
  262.3 3.9 copy.98
  266.5 40.3 %attn_bwd.1 = bf16[576,2048]{1,0:T(8,128)(2,1)S(1)} custom-call(bf16[2048,768]{1,0:T(8,128)(2,1)} %get-tuple-element.47.da_ref, bf16[192,768]{1,0:T(8,128)(2,1)S(1)} %copy-done.21, bf16[576,2048]{1,0:T(8,128)(2,1)} %copy-done.23, bf16[192,2048]{1,0:T(8,128)(2,1)} %get-tuple-element.37.refs_0_.ot_ref, f32[8,2048]{1,0:T(8,128)S(1)} %copy-done.25, ...), custom_call_target="tpu_custom_call" | custom-call | flops 40000000000 | bytes 10000000 | tf_op jit(solution)/shard_map/attn_bwd/pallas_call | solution.py:215
  311.8 3.0 add_convert_fusion.5
  315.4 4.9 %multiply_reduce_fusion = (f32[768]{0:T(1024)S(1)}, f32[768,576]{0,1:T(8,128)S(1)}) fusion(bf16[768,576]{0,1:T(8,128)(2,1)S(1)} %copy-done.14, bf16[576,2048]{1,0:T(8,128)(2,1)} %copy-done.22, bf16[2048,768]{1,0:T(8,128)(2,1)} %get-tuple-element.52), kind=kOutput, calls=%fused_computation.14 | convolution fusion | flops 1813265664 | bytes 8162304 | tf_op jit(solution)/shard_map/dot_general | solution.py:732
  326.0 26.4 %collective-permute-done.9 = bf16[2048,384]{1,0:T(8,128)(2,1)} collective-permute-done((bf16[2048,384]{1,0:T(8,128)(2,1)}, bf16[2048,384]{1,0:T(8,128)(2,1)}, u32[]{:S(2)}, u32[]{:S(2)}) %collective-permute-start.9) | collective-permute-done | bytes 1572896 | tf_op jit(solution)/shard_map/ppermute | solution.py:51
  360.1 25.0 %collective-permute-done.23 = f32[1,768]{1,0:T(1,128)S(1)} collective-permute-done((f32[1,768]{1,0:T(1,128)S(1)}, f32[1,768]{1,0:T(1,128)S(1)}, u32[]{:S(2)}, u32[]{:S(2)}) %collective-permute-start.23) | collective-permute-done | bytes 3104 | tf_op jit(solution)/shard_map/ppermute | solution.py:51
  406.3 11.6 %output.1 = f32[2048,768]{1,0:T(8,128)} custom-call(s32[2]{0:T(128)S(1)} %pad_add_fusion.idx_ref, bf16[2048,384]{1,0:T(8,128)(2,1)S(1)} %add_convert_fusion.4.mine_ref, bf16[2048,384]{1,0:T(8,128)(2,1)} %collective-permute-done.10.theirs_ref, f32[2048,768]{1,0:T(8,128)} %get-tuple-element.43.x1_ref, bf16[2048,768]{1,0:T(8,128)(2,1)} %get-tuple-element.38.h2_ref, ...), custom_call_target="tpu_custom_call" | custom-call | flops 20000000 | bytes 22000000 | tf_op jit(solution)/shard_map/output/pallas_call | solution.py:595
  419.0 7.0 %collective-permute-done.29 = f32[48,768]{1,0:T(8,128)S(1)} collective-permute-done((f32[48,768]{1,0:T(8,128)S(1)}, f32[48,768]{1,0:T(8,128)S(1)}, u32[]{:S(2)}, u32[]{:S(2)}) %collective-permute-start.29) | collective-permute-done | bytes 147488 | tf_op jit(solution)/shard_map/ppermute | solution.py:51
  436.1 10.4 %last.1 = f32[2048,768]{1,0:T(8,128)} custom-call(s32[2]{0:T(128)S(1)} %pad_add_fusion.idx_ref, bf16[2048,384]{1,0:T(8,128)(2,1)S(1)} %add_convert_fusion.mine_ref, bf16[2048,384]{1,0:T(8,128)(2,1)} %collective-permute-done.21.theirs_ref, bf16[2048,768]{1,0:T(8,128)(2,1)} %x_ref.5, f32[2048,768]{1,0:T(8,128)} %get-tuple-element.50.dx1_ref, ...), custom_call_target="tpu_custom_call" | custom-call | flops 20000000 | bytes 20000000 | tf_op jit(solution)/shard_map/last/pallas_call | solution.py:634
  (213 shorter events, 90.2 us)
Async XLA Ops:
  7.2 192.6 %reduce-scatter.17.cloned.1.call-start = ((), (), s32[]{:S(2)}) async-start(), calls=%async_computation.7 | async-start | bytes 2359296 | tf_op jit(solution)/shard_map/reduce_scatter | solution.py:739
  55.2 21.6 %collective-permute-start.1 = (bf16[192,2048]{1,0:T(8,128)(2,1)}, bf16[192,2048]{1,0:T(8,128)(2,1)S(1)}, u32[]{:S(2)}, u32[]{:S(2)}) collective-permute-start(bf16[192,2048]{1,0:T(8,128)(2,1)} %get-tuple-element.37.refs_0_.ot_ref), channel_id=1, source_target_pairs={{0,2},{1,3},{2,0},{3,1},{4,6},{5,7},{6,4},{7,5},{8,10},{9,11},{10,... | collective-permute-start | bytes 2359304 | tf_op jit(solution)/shard_map/ppermute | solution.py:51
  59.8 53.0 %collective-permute-start.6 = (bf16[768,1024]{1,0:T(8,128)(2,1)}, bf16[768,1024]{1,0:T(8,128)(2,1)}, u32[]{:S(2)}, u32[]{:S(2)}) collective-permute-start(bf16[768,1024]{1,0:T(8,128)(2,1)} %bitcast.33.refs_0_), channel_id=1, source_target_pairs={{0,4},{4,0},{1,5},{5,1},{2,6},{6,2},{3,7},{7,3},{8,12},{12,8},{9,1... | collective-permute-start | bytes 4718600 | tf_op jit(solution)/shard_map/ppermute | solution.py:51
  61.3 21.0 %collective-permute-start.4 = (bf16[192,768]{1,0:T(8,128)(2,1)S(1)}, bf16[192,768]{1,0:T(8,128)(2,1)S(1)}, u32[]{:S(2)}, u32[]{:S(2)}) collective-permute-start(bf16[192,768]{1,0:T(8,128)(2,1)S(1)} %copy-done.20), channel_id=1, source_target_pairs={{0,2},{1,3},{2,0},{3,1},{4,6},{5,7},{6,4},{7,5},{8,10},{9,11},{10,... | collective-permute-start | bytes 884744 | tf_op jit(solution)/shard_map/ppermute | solution.py:51
  61.8 26.1 %collective-permute-start = (bf16[192,2048]{1,0:T(8,128)(2,1)}, bf16[192,2048]{1,0:T(8,128)(2,1)}, u32[]{:S(2)}, u32[]{:S(2)}) collective-permute-start(bf16[192,2048]{1,0:T(8,128)(2,1)} %get-tuple-element.37.refs_0_.ot_ref), channel_id=1, source_target_pairs={{0,1},{1,0},{2,3},{3,2},{4,5},{5,4},{6,7},{7,6},{8,9},{9,8},{10,11... | collective-permute-start | bytes 2359304 | tf_op jit(solution)/shard_map/ppermute | solution.py:51
  76.9 11.1 %collective-permute-start.2 = (bf16[192,2048]{1,0:T(8,128)(2,1)S(1)}, bf16[192,2048]{1,0:T(8,128)(2,1)}, u32[]{:S(2)}, u32[]{:S(2)}) collective-permute-start(bf16[192,2048]{1,0:T(8,128)(2,1)S(1)} %collective-permute-done.1.refs_2_), channel_id=1, source_target_pairs={{0,1},{1,0},{2,3},{3,2},{4,5},{5,4},{6,7},{7,6},{8,9},{9,8},{10,11... | collective-permute-start | bytes 2359304 | tf_op jit(solution)/shard_map/ppermute | solution.py:51
  82.3 30.5 %collective-permute-start.7 = (bf16[512,768]{1,0:T(8,128)(2,1)S(1)}, bf16[512,768]{1,0:T(8,128)(2,1)}, u32[]{:S(2)}, u32[]{:S(2)}) collective-permute-start(bf16[512,768]{1,0:T(8,128)(2,1)S(1)} %bitcast.69), channel_id=1, source_target_pairs={{0,4},{4,0},{1,5},{5,1},{2,6},{6,2},{3,7},{7,3},{8,12},{12,8},{9,1... | collective-permute-start | bytes 2359304 | tf_op jit(solution)/shard_map/ppermute | solution.py:51
  146.9 107.0 %reduce-scatter.15.cloned.1.call-start = ((), (), s32[]{:S(2)}) async-start(), calls=%async_computation.6 | async-start | bytes 4718592 | tf_op jit(solution)/shard_map/reduce_scatter | solution.py:737
  158.5 231.9 %reduce-scatter.25.cloned.1.call-start = ((), (), s32[]{:S(2)}) async-start(), calls=%async_computation.11 | async-start | bytes 983040
  162.7 36.5 %collective-permute-start.12 = (bf16[2048,384]{1,0:T(8,128)(2,1)S(1)}, bf16[2048,384]{1,0:T(8,128)(2,1)S(1)}, u32[]{:S(2)}, u32[]{:S(2)}) collective-permute-start(bf16[2048,384]{1,0:T(8,128)(2,1)S(1)} %add_convert_fusion.3), channel_id=1, source_target_pairs={{0,2},{1,3},{2,0},{3,1},{4,6},{5,7},{6,4},{7,5},{8,10},{9,11},{10,... | collective-permute-start | bytes 4718600 | tf_op jit(solution)/shard_map/ppermute | solution.py:51
  199.6 21.6 %collective-permute-start.13 = (bf16[2048,384]{1,0:T(8,128)(2,1)S(1)}, bf16[2048,384]{1,0:T(8,128)(2,1)}, u32[]{:S(2)}, u32[]{:S(2)}) collective-permute-start(bf16[2048,384]{1,0:T(8,128)(2,1)S(1)} %add_convert_fusion.2.mine_ref), channel_id=1, source_target_pairs={{0,1},{1,0},{2,3},{3,2},{4,5},{5,4},{6,7},{7,6},{8,9},{9,8},{10,11... | collective-permute-start | bytes 4718600 | tf_op jit(solution)/shard_map/ppermute | solution.py:51
  207.1 223.8 %reduce-scatter.21.cloned.1.call-start = ((), (), s32[]{:S(2)}) async-start(), calls=%async_computation.9 | async-start | bytes 884736
  244.7 187.8 %reduce-scatter.23.cloned.1.call-start = ((), (), s32[]{:S(2)}) async-start(), calls=%async_computation.10 | async-start | bytes 1966080
  253.9 57.9 %collective-permute-start.8 = (bf16[2048,384]{1,0:T(8,128)(2,1)}, bf16[2048,384]{1,0:T(8,128)(2,1)}, u32[]{:S(2)}, u32[]{:S(2)}) collective-permute-start(bf16[2048,384]{1,0:T(8,128)(2,1)} %get-tuple-element.42), channel_id=1, source_target_pairs={{0,1},{1,0},{2,3},{3,2},{4,5},{5,4},{6,7},{7,6},{8,9},{9,8},{10,11... | collective-permute-start | bytes 4718600 | tf_op jit(solution)/shard_map/ppermute | solution.py:51
  266.2 180.4 %reduce-scatter.19.cloned.1.call-start = ((), (), s32[]{:S(2)}) async-start(), calls=%async_computation.8 | async-start | bytes 2211840
  311.2 10.9 %collective-permute-start.19 = (bf16[2048,384]{1,0:T(8,128)(2,1)}, bf16[2048,384]{1,0:T(8,128)(2,1)}, u32[]{:S(2)}, u32[]{:S(2)}) collective-permute-start(bf16[2048,384]{1,0:T(8,128)(2,1)} %constant_dynamic-slice_fusion), channel_id=1, source_target_pairs={{0,1},{1,0},{2,3},{3,2},{4,5},{5,4},{6,7},{7,6},{8,9},{9,8},{10,11... | collective-permute-start | bytes 4718600 | tf_op jit(solution)/shard_map/ppermute | solution.py:51
  314.8 37.6 %collective-permute-start.9 = (bf16[2048,384]{1,0:T(8,128)(2,1)}, bf16[2048,384]{1,0:T(8,128)(2,1)}, u32[]{:S(2)}, u32[]{:S(2)}) collective-permute-start(bf16[2048,384]{1,0:T(8,128)(2,1)} %add_convert_fusion.5), channel_id=1, source_target_pairs={{0,2},{1,3},{2,0},{3,1},{4,6},{5,7},{6,4},{7,5},{8,10},{9,11},{10,... | collective-permute-start | bytes 4718600 | tf_op jit(solution)/shard_map/ppermute | solution.py:51
  324.5 62.2 %collective-permute-start.20 = (bf16[2048,384]{1,0:T(8,128)(2,1)S(1)}, bf16[2048,384]{1,0:T(8,128)(2,1)S(1)}, u32[]{:S(2)}, u32[]{:S(2)}) collective-permute-start(bf16[2048,384]{1,0:T(8,128)(2,1)S(1)} %add_convert_fusion.1), channel_id=1, source_target_pairs={{0,2},{1,3},{2,0},{3,1},{4,6},{5,7},{6,4},{7,5},{8,10},{9,11},{10,... | collective-permute-start | bytes 4718600 | tf_op jit(solution)/shard_map/ppermute | solution.py:51
  354.7 49.4 %collective-permute-start.10 = (bf16[2048,384]{1,0:T(8,128)(2,1)S(1)}, bf16[2048,384]{1,0:T(8,128)(2,1)}, u32[]{:S(2)}, u32[]{:S(2)}) collective-permute-start(bf16[2048,384]{1,0:T(8,128)(2,1)S(1)} %add_convert_fusion.4.mine_ref), channel_id=1, source_target_pairs={{0,1},{1,0},{2,3},{3,2},{4,5},{5,4},{6,7},{7,6},{8,9},{9,8},{10,11... | collective-permute-start | bytes 4718600 | tf_op jit(solution)/shard_map/ppermute | solution.py:51
  358.2 27.0 %collective-permute-start.23 = (f32[1,768]{1,0:T(1,128)S(1)}, f32[1,768]{1,0:T(1,128)S(1)}, u32[]{:S(2)}, u32[]{:S(2)}) collective-permute-start(f32[1,768]{1,0:T(1,128)S(1)} %reshape_add_fusion), channel_id=1, source_target_pairs={{0,2},{1,3},{2,0},{3,1},{4,6},{5,7},{6,4},{7,5},{8,10},{9,11},{10,... | collective-permute-start | bytes 9224 | tf_op jit(solution)/shard_map/ppermute | solution.py:51
  358.8 37.9 %collective-permute-start.27 = (f32[48,768]{1,0:T(8,128)S(1)}, f32[48,768]{1,0:T(8,128)}, u32[]{:S(2)}, u32[]{:S(2)}) collective-permute-start(f32[48,768]{1,0:T(8,128)S(1)} %pad_dynamic-update-slice_fusion), channel_id=1, source_target_pairs={{0,4},{4,0},{1,5},{5,1},{2,6},{6,2},{3,7},{7,3},{8,12},{12,8},{9,1... | collective-permute-start | bytes 442376 | tf_op jit(solution)/shard_map/ppermute | solution.py:51
  387.2 49.0 %collective-permute-start.21 = (bf16[2048,384]{1,0:T(8,128)(2,1)S(1)}, bf16[2048,384]{1,0:T(8,128)(2,1)}, u32[]{:S(2)}, u32[]{:S(2)}) collective-permute-start(bf16[2048,384]{1,0:T(8,128)(2,1)S(1)} %add_convert_fusion.mine_ref), channel_id=1, source_target_pairs={{0,1},{1,0},{2,3},{3,2},{4,5},{5,4},{6,7},{7,6},{8,9},{9,8},{10,11... | collective-permute-start | bytes 4718600 | tf_op jit(solution)/shard_map/ppermute | solution.py:51
  394.1 23.8 %collective-permute-start.26 = (f32[1,768]{1,0:T(1,128)S(1)}, f32[1,768]{1,0:T(1,128)S(1)}, u32[]{:S(2)}, u32[]{:S(2)}) collective-permute-start(f32[1,768]{1,0:T(1,128)S(1)} %add.114), channel_id=1, source_target_pairs={{0,16},{8,24},{16,0},{24,8},{1,17},{9,25},{17,1},{25,9},{2,18},{10... | collective-permute-start | bytes 9224 | tf_op jit(solution)/shard_map/ppermute | solution.py:51
  397.6 20.3 %collective-permute-start.28 = (f32[48,768]{1,0:T(8,128)S(1)}, f32[48,768]{1,0:T(8,128)S(1)}, u32[]{:S(2)}, u32[]{:S(2)}) collective-permute-start(f32[48,768]{1,0:T(8,128)S(1)} %add.116), channel_id=1, source_target_pairs={{0,8},{8,0},{16,24},{24,16},{1,9},{9,1},{17,25},{25,17},{2,10},{10... | collective-permute-start | bytes 442376 | tf_op jit(solution)/shard_map/ppermute | solution.py:51
  (49 other events, 795.5 us)
Sparse Core Ops, SparseCore 0:
  147.0 26.3 reduce-scatter.16
  175.7 43.3 reduce-scatter.14
  221.4 23.3 reduce-scatter.24
  247.9 61.8 reduce-scatter.20
  312.1 34.2 reduce-scatter.22
  350.7 65.6 reduce-scatter.18
